TPU v7x, 256 devices: a whole 4x4x8 slice. The times are simulated.
256 devices in a mesh: px: 16 (over x_lo, z), py: 16 (over y, x_hi, core).
Axes of the slice: x: 4 (x_hi: 2, x_lo: 2; x = x_hi * 2 + x_lo), y: 4, z: 8, core: 2. Of those that a mesh axis runs over, the one named last changes fastest.
Arguments:
- inputs: float32 [64, 256, 8192], P(None, 'px', 'py'), may hold values from -6 to 6
- pre_act: float32 [64, 256, 8192], P(None, 'px', 'py'), may hold values from -8 to 8
- cotangent: float32 [64, 256, 8192], P(None, 'px', 'py'), may hold values from -6 to 6
- mix_weight: float32 [64, 64], replicated, may hold values from -0.75 to 0.75
- spectral_weight: float32 [32, 32, 8, 64, 128], P('py', 'px'), may hold values from -6 to 6
Outputs:
- input_grad: float32 [64, 256, 8192], P(None, 'px', 'py')
- spectral_grad: float32 [32, 32, 8, 64, 128], P('py', 'px')
- mix_grad: float32 [64, 64], replicated
All inputs are finite; a program needn't handle non-finite values.
Results may differ from a plain program's by a relative error of at most 0.0001.
Values sent between devices are 32-bit elements; how exact they have to be, the bound alone decides.
No kernel may reach another device: no remote copies, remote signals or barrier semaphores. Data moves between devices by JAX's collectives and lax.ppermute only.
A program may use at most 192 MiB of HBM per device.

v0:
```python
import math

import jax
import jax.numpy as jnp
import ml_dtypes
import numpy as np
from jax import lax
from jax.experimental import pallas as pl
from jax.experimental.pallas import tpu as pltpu
from jax.sharding import PartitionSpec as P

C = 64
NX = 256
NY = 256
NZ = 32
MZ = 8
CELLS = NX * NY * NZ
N = 16
F32 = jnp.float32
BF16 = jnp.bfloat16


def pair(table):
    high = table.astype(ml_dtypes.bfloat16)
    low = (table - high.astype(np.float64)).astype(high.dtype)
    return high, low


def frequency(index):
    return np.where(index < 16, index, index - 32)


def angle(a, b, length):
    return 2.0 * np.pi / length * np.mod(a * b, length)


def depth_forward():
    k, z = np.arange(8)[:, None], np.arange(32)[None, :]
    t = angle(k, z, 32)
    parts = np.stack([np.cos(t), -np.sin(t)], 1)
    return np.einsum("krz,ab->krabz", parts, np.eye(16)).reshape(256, 512)


def depth_inverse():
    return depth_forward().reshape(4, 2, 2, 16, 512).transpose(1, 0, 2, 3, 4).reshape(256, 512)


def second_forward():
    q = np.arange(32)
    t = angle(frequency(q)[:, None], np.arange(256)[None, :], 256)
    c, s = np.cos(t), np.sin(t)
    full = np.stack([np.stack([c, s], 1), np.stack([-s, c], 1)], 0)
    full = full.reshape(2, 16, 2, 2, 16, 16)
    return full.transpose(0, 2, 1, 4, 3, 5).reshape(64, 512)


def second_inverse():
    q = np.arange(32)
    t = angle(frequency(q)[:, None], np.arange(256)[None, :], 256)
    c, s = np.cos(t), np.sin(t)
    full = np.stack([np.stack([c, s], 0), np.stack([-s, c], 0)], 0)
    full = full.reshape(2, 2, 16, 2, 16, 16)
    return full.transpose(4, 1, 5, 0, 3, 2).reshape(512, 64)


def first_twiddle():
    t = angle(np.arange(16)[:, None], np.arange(128)[None, :] % 16, 256)
    return np.concatenate([np.cos(t), np.sin(t)], 0).astype(np.float32)


def first_halves():
    t = angle(np.arange(2)[:, None], np.arange(16)[None, :], 16)
    c, s = np.cos(t), np.sin(t)
    full = np.stack([np.stack([c, -s], 1), np.stack([s, c], 1)], 1)
    return np.einsum("hsrx,ab->hsarbx", full, np.eye(8)).reshape(32, 256)


def first_inverse():
    p = np.arange(32)
    t = angle(frequency(p)[:, None], np.arange(256)[None, :], 256)
    full = np.stack([np.cos(t), np.sin(t)], 0).reshape(2, 16, 2, 256)
    return full.transpose(0, 2, 1, 3).reshape(64, 256)


def split(values):
    high = values.astype(BF16)
    low = (values - high.astype(F32)).astype(BF16)
    return high, low


def dot(a, b, dims=((1,), (0,))):
    return lax.dot_general(a, b, (dims, ((), ())), preferred_element_type=F32)


def dot3(a, b, dims=((1,), (0,))):
    return dot(a[0], b[0], dims) + (dot(a[0], b[1], dims) + dot(a[1], b[0], dims))


def lanes(shape):
    return lax.broadcasted_iota(jnp.int32, shape, len(shape) - 1)


def transpose_groups(blocks, width):
    blocks = list(blocks)
    count = len(blocks)
    group = lanes(blocks[0].shape) // width
    step = 1
    while step < count:
        upper = (group & step) != 0
        for i in range(count):
            if i & step:
                continue
            a, b = blocks[i], blocks[i | step]
            blocks[i] = jnp.where(upper, pltpu.roll(b, step * width, 1), a)
            blocks[i | step] = jnp.where(upper, b, pltpu.roll(a, 128 - step * width, 1))
        step *= 2
    return blocks


def fft(parts):
    count = len(parts)
    if count == 1:
        return parts
    even, odd = fft(parts[0::2]), fft(parts[1::2])
    out = [None] * count
    for j in range(count // 2):
        er, ei = even[j]
        orr, oi = odd[j]
        if j == 0:
            tr, ti = orr, oi
        elif 4 * j == count:
            tr, ti = oi, -orr
        else:
            c, s = math.cos(2 * math.pi * j / count), math.sin(2 * math.pi * j / count)
            tr, ti = orr * c + oi * s, oi * c - orr * s
        out[j] = (er + tr, ei + ti)
        out[j + count // 2] = (er - tr, ei - ti)
    return out


def start_kernel(x_ref, pre_ref, cot_ref, dh_ref, dl_ref, grad_ref, out_ref):
    v = pre_ref[...]
    cumulative = 0.5 * (1.0 + lax.erf(v * (1.0 / math.sqrt(2.0))))
    density = jnp.exp(-0.5 * v * v) * (1.0 / math.sqrt(2.0 * math.pi))
    grad = cot_ref[...] * (cumulative + v * density)
    grad_ref[...] = grad
    table = (dh_ref[...], dl_ref[...])
    for i in range(x_ref.shape[1]):
        rows = jnp.concatenate(
            [x_ref[c, i] for c in range(4)] + [grad[c, i] for c in range(4)], axis=0
        )
        out_ref[i] = dot3(table, split(rows), ((1,), (1,)))


def second_kernel(in_ref, th_ref, tl_ref, out_ref):
    both = jnp.concatenate([th_ref[...], tl_ref[...]], axis=0)
    for k in range(8):
        rows = jnp.concatenate([in_ref[s, 32 * k : 32 * k + 32, :] for s in range(16)], axis=0)
        high, low = split(rows)
        two = dot(both, high)
        done = two[:64] + (two[64:] + dot(th_ref[...], low))
        for ri in range(2):
            for q in range(2):
                j = 2 * ri + q
                out_ref[pl.ds(ri * 16 + k * 2 + q, 16, stride=32), :] = done[16 * j : 16 * j + 16]


def first_kernel(in_ref, tw_ref, bh_ref, bl_ref, mix_ref, out_ref):
    parts = [(in_ref[32 * s : 32 * s + 16], in_ref[32 * s + 16 : 32 * s + 32]) for s in range(16)]
    rows = []
    for r, (re, im) in enumerate(fft(parts)):
        c, s = tw_ref[r : r + 1], tw_ref[16 + r : 17 + r]
        rows.append(jnp.concatenate([re * c + im * s, im * c - re * s], axis=1))
    data = split(jnp.concatenate(rows, axis=0))
    done = dot3((bh_ref[...], bl_ref[...]), data, ((1,), (1,)))
    lane = lanes((16, 128))
    for h in range(2):
        for b in range(8):
            tile = done[16 * h : 16 * h + 16, 128 * (b // 4) : 128 * (b // 4) + 128]
            if b % 4:
                tile = pltpu.roll(tile, 128 - 32 * (b % 4), 1)
            d = 8 * h + b
            mix = mix_ref[16 * (d // 4) : 16 * (d // 4) + 16]
            shift = (32 - 16 * (d % 4)) % 128
            if shift:
                mix = pltpu.roll(mix, shift, 1)
            out_ref[16 * d : 16 * d + 16] = jnp.where(lane < 32, tile, mix)


def swap_halves(b1):
    turned = pltpu.roll(b1, 64, 1)
    return jnp.where(lanes(b1.shape) < 64, turned, -turned)


def mode_kernel(in_ref, w_ref, out_ref, xr_ref, xi_ref, b1_ref, mix_ref):
    def field(ri, f):
        return jnp.concatenate(
            [in_ref[pl.ds(8 * ri + 4 * f + c, 16, stride=16), :] for c in range(4)], axis=0
        )

    spread = jnp.concatenate([field(0, 1), field(1, 1)], axis=0).T[:32]
    mode = lax.broadcasted_iota(jnp.int32, (32, 128), 0)
    b1 = spread * jnp.where((mode // 2) % 8 == 0, 1.0 / CELLS, 2.0 / CELLS)
    b2 = swap_halves(b1)
    lane = lanes((64, 128))
    total = jnp.zeros((64, 128), F32)
    for m in range(32):
        p, k, q = m // 16, (m // 2) % 8, m % 2
        at = ((p * 2 + q) * 8 + k) * 64
        weight = w_ref[at : at + 64]
        place = q + 4 * (k // 2) + 16 * p + 64 * (k % 2)
        real = jnp.sum(weight * b1[m : m + 1], axis=1, keepdims=True)
        imag = jnp.sum(weight * b2[m : m + 1], axis=1, keepdims=True)
        total = jnp.where(lane == place, real, total)
        total = jnp.where(lane == place + 2, imag, total)
    for c in range(4):
        out_ref[pl.ds(c, 16, stride=4), :] = total[16 * c : 16 * c + 16]
    xr_ref[...] = field(0, 0)
    xi_ref[...] = field(1, 0)
    b1_ref[...] = b1
    mix = in_ref[0:16]
    for s in range(1, 16):
        mix = mix + in_ref[16 * s : 16 * s + 16]
    mix_ref[...] = jnp.where(lanes((8, 128)) < 48, mix[:8], pltpu.roll(mix[8:], 16, 1))


def outer_kernel(xr_ref, xi_ref, b1_ref, out_ref):
    xr, xi, b1 = xr_ref[...], xi_ref[...], b1_ref[...]
    b2 = swap_halves(b1)
    for m in range(32):
        p, k, q = m // 16, (m // 2) % 8, m % 2
        at = ((p * 2 + q) * 8 + k) * 64
        out_ref[at : at + 64] = xr[:, m : m + 1] * b1[m : m + 1] + xi[:, m : m + 1] * b2[m : m + 1]


def first_back_kernel(in_ref, t_ref, mix_ref, out_ref):
    parts = [in_ref[pl.ds(c, 16, stride=4), :] for c in range(4)]
    lane = lanes((16, 128))
    rows = []
    for p in range(2):
        merged = None
        for c in range(4):
            shift = (16 * (c - p)) % 128
            moved = pltpu.roll(parts[c], shift, 1) if shift else parts[c]
            merged = moved if merged is None else jnp.where((lane // 16) % 4 == c, moved, merged)
        rows.append(merged)
    re = jnp.concatenate(rows, axis=0)
    turned = jnp.where(
        (lanes((32, 128)) // 2) % 2 == 0, -pltpu.roll(re, 126, 1), pltpu.roll(re, 2, 1)
    )
    high, low = split(jnp.concatenate([re, turned], axis=0))
    done = dot(jnp.concatenate([high, high, low], axis=0), t_ref[...], ((0,), (0,)))
    mix = mix_ref[...]
    for t in range(2):
        blocks = [done[16 * b : 16 * b + 16, 128 * t : 128 * t + 128] for b in range(8)]
        for g, block in enumerate(transpose_groups(blocks, 16)):
            out_ref[8 * t + g, 0:16, :] = block
            out_ref[8 * t + g, 16:24, :] = mix


def second_back_kernel(in_ref, t_ref, out_ref):
    for k in range(4):
        rows = jnp.concatenate(
            [in_ref[pl.ds(4 * k + j, 16, stride=24), :] for j in range(4)], axis=0
        )
        high, low = split(rows)
        done = dot(t_ref[...], jnp.concatenate([high, high, low], axis=0))
        for y in range(16):
            out_ref[y, 32 * k : 32 * k + 32, :] = done[32 * y : 32 * y + 32]
    mix = in_ref[16:24]
    for s in range(1, 16):
        mix = mix + in_ref[24 * s + 16 : 24 * s + 24]
    lane = lanes((8, 128))
    for y in range(16):
        out_ref[y, 16:24, :] = jnp.where(lane < 64, mix, out_ref[y, 16:24, :])


def end_kernel(in_ref, mixed_ref, direct_ref, dh_ref, dl_ref, out_ref, mix_ref):
    table = (dh_ref[...], dl_ref[...])
    for i in range(in_ref.shape[0]):
        turned = in_ref[i].T
        rows = jnp.concatenate([turned[:64], turned[64:]], axis=1)
        done = dot3(split(rows), table)
        for c in range(4):
            out_ref[c, i] = direct_ref[c, i] + done[16 * c : 16 * c + 16]

    @pl.when(pl.program_id(0) == 0)
    def _():
        lane = lanes((8, 128))
        scale = 1.0 / math.sqrt(CELLS)
        for block in range(4):
            for half in range(2):
                total = None
                for o in range(4):
                    part = mixed_ref[4 * block + o]
                    shift = (16 * o - 32 - 16 * half) % 128
                    part = pltpu.roll(part, shift, 1) if shift else part
                    total = part if total is None else jnp.where(lane // 16 == o, part, total)
                at = 16 * block + 8 * half
                mix_ref[at : at + 8, :] = total[:, :64] * scale


def side_kernel(x_ref, grad_ref, weight_ref, direct_ref, mix_ref):
    high, low = split(weight_ref[...])
    weight = jnp.concatenate([high, low, high], axis=1)
    total = jnp.zeros((64, 64), F32)
    for x in range(16):
        field = split(x_ref[:, x, :])
        gh, gl = split(grad_ref[:, x, :])
        total = total + dot3(field, (gh, gl), ((1,), (1,)))
        direct_ref[:, x, :] = dot(weight, jnp.concatenate([gh, gh, gl], axis=0))
    mix_ref[...] = jnp.concatenate([total, total], axis=1)


def params(mebibytes):
    return pltpu.CompilerParams(vmem_limit_bytes=mebibytes << 20)


def whole(count):
    return [pl.BlockSpec(memory_space=pltpu.VMEM)] * count


def struct(*shape):
    return jax.ShapeDtypeStruct(shape, F32)


def call(body, outs, args, mebibytes=16, cost=None):
    many = isinstance(outs, tuple)
    return pl.pallas_call(
        body,
        out_shape=outs,
        in_specs=whole(len(args)),
        out_specs=tuple(whole(len(outs))) if many else whole(1)[0],
        compiler_params=params(mebibytes),
        cost_estimate=cost,
    )(*args)


def exchange(values, axis):
    return lax.all_to_all(values, axis, split_axis=0, concat_axis=0, tiled=True)


def stacked(table):
    high, low = pair(table)
    return np.concatenate([high, low, high], axis=1)


def per_device(inputs, pre_act, cotangent, mix_weight, spectral_weight):
    steps, per = 4, 4
    field_spec = pl.BlockSpec((4, per, 16, 512), lambda i: (0, i, 0, 0))
    table_spec = pl.BlockSpec((256, 512), lambda i: (0, 0))
    shaped = [a.reshape(4, 16, 16, 512) for a in (inputs, pre_act, cotangent)]
    grad_pre, depth = pl.pallas_call(
        start_kernel,
        grid=(steps,),
        out_shape=(struct(4, 16, 16, 512), struct(16, 256, 128)),
        in_specs=[field_spec] * 3 + [table_spec] * 2,
        out_specs=(field_spec, pl.BlockSpec((per, 256, 128), lambda i: (i, 0, 0))),
        compiler_params=params(32),
    )(*shaped, *map(jnp.asarray, pair(depth_forward())))

    depth = exchange(depth, "py")
    direct, mix = call(
        side_kernel,
        (struct(64, 16, 512), struct(64, 128)),
        (inputs, grad_pre.reshape(64, 16, 512), mix_weight),
        24,
        pl.CostEstimate(flops=1 << 30, bytes_accessed=6 << 20, transcendentals=0),
    )
    along_second = call(
        second_kernel, struct(512, 128), (depth, *map(jnp.asarray, pair(second_forward()))), 16
    )
    along_second = exchange(along_second.reshape(16, 32, 128), "px").reshape(512, 128)
    along_first = call(
        first_kernel,
        struct(256, 128),
        (along_second, jnp.asarray(first_twiddle()), *map(jnp.asarray, pair(first_halves())), mix),
    )
    spectra = exchange(along_first.reshape(16, 16, 128), "py").reshape(256, 128)
    mode_back, xr, xi, b1, mix = call(
        mode_kernel,
        (struct(64, 128), struct(64, 128), struct(64, 128), struct(32, 128), struct(8, 128)),
        (spectra, spectral_weight.reshape(2048, 128)),
    )
    mode_back = exchange(mode_back.reshape(16, 4, 128), "py").reshape(64, 128)
    spectral_grad = call(
        outer_kernel,
        struct(2048, 128),
        (xr, xi, b1),
        16,
        pl.CostEstimate(flops=1 << 20, bytes_accessed=1 << 20, transcendentals=0),
    ).reshape(spectral_weight.shape)
    first_high, first_low = pair(first_inverse())
    first_table = np.concatenate([first_high, first_low, first_high], axis=0)
    first_back = call(
        first_back_kernel, struct(16, 24, 128), (mode_back, jnp.asarray(first_table), mix)
    )
    first_back = exchange(first_back, "px").reshape(384, 128)
    second_back = call(
        second_back_kernel,
        struct(16, 128, 128),
        (first_back, jnp.asarray(stacked(second_inverse()))),
    )
    gathered = exchange(second_back, "py")
    input_grad, mix_grad = pl.pallas_call(
        end_kernel,
        grid=(steps,),
        out_shape=(struct(4, 16, 16, 512), struct(64, 64)),
        in_specs=[
            pl.BlockSpec((per, 128, 128), lambda i: (i, 0, 0)),
            pl.BlockSpec((16, 8, 128), lambda i: (0, 2, 0)),
            field_spec,
            table_spec,
            table_spec,
        ],
        out_specs=(field_spec, pl.BlockSpec((64, 64), lambda i: (0, 0))),
        compiler_params=params(24),
    )(
        gathered,
        gathered,
        direct.reshape(4, 16, 16, 512),
        *map(jnp.asarray, pair(depth_inverse())),
    )
    return (input_grad.reshape(inputs.shape), spectral_grad, mix_grad)


def solution(mesh):
    placed = (
        P(None, "px", "py"),
        P(None, "px", "py"),
        P(None, "px", "py"),
        P(),
        P("py", "px", None, None, None),
    )
    return jax.shard_map(
        per_device,
        mesh=mesh,
        in_specs=placed,
        out_specs=(P(None, "px", "py"), P("py", "px", None, None, None), P()),
        check_vma=False,
    )
```

profile of v0, /device:TPU:1, one launch (start us, length us, event | category | flops | bytes accessed | tf_op | source)
XLA Modules:
  0.0 146.5 jit_solution(11280959580279726091)
XLA Ops:
  0.6 1.6 %copy-done = f32[64,16,512]{2,1,0:T(8,128)S(1)} copy-done((f32[64,16,512]{2,1,0:T(8,128)S(1)}, f32[64,16,512]{2,1,0:T(8,128)}, u32[]{:S(2)}) %copy-start) | copy-done | bytes 2097176
  2.2 1.6 %copy-done.2 = f32[64,16,512]{2,1,0:T(8,128)S(1)} copy-done((f32[64,16,512]{2,1,0:T(8,128)S(1)}, f32[64,16,512]{2,1,0:T(8,128)}, u32[]{:S(2)}) %copy-start.2) | copy-done | bytes 2097176
  3.8 1.6 %copy-done.3 = f32[64,16,512]{2,1,0:T(8,128)S(1)} copy-done((f32[64,16,512]{2,1,0:T(8,128)S(1)}, f32[64,16,512]{2,1,0:T(8,128)}, u32[]{:S(2)}) %copy-start.3) | copy-done | bytes 2097176
  5.4 0.9 copy-done.12
  6.4 0.9 copy-done.13
  7.3 4.6 %shard_map.175 = (f32[4,16,16,512]{3,2,1,0:T(8,128)S(1)}, f32[16,256,128]{2,1,0:T(8,128)S(1)}) custom-call(f32[4,16,16,512]{3,2,1,0:T(8,128)S(1)} %bitcast.15, f32[4,16,16,512]{3,2,1,0:T(8,128)S(1)} %bitcast.16, f32[4,16,16,512]{3,2,1,0:T(8,128)S(1)} %bitcast.17, bf16[256,512]{1,0:T(8,128)(2,1)S(1)} %copy-done.13, bf16[256,512]{1,0:T(8,128)(2,1)S(1)} %copy-done.12), custom_call_target="tpu_custom_call" | custom-call | tf_op jit(solution)/shard_map/pallas_call | solution.py:353
  12.0 0.0 copy-start.15
  12.0 0.0 copy-start.16
  12.0 36.5 %all_to_all.30.in_ref = f32[16,256,128]{2,1,0:T(8,128)S(1)} all-to-all(f32[16,256,128]{2,1,0:T(8,128)S(1)} %get-tuple-element.14), channel_id=1, replica_groups=mesh['px'=16,'py'=16] {'py'}, dimensions={0} | all-to-all | bytes 4194304 | tf_op jit(solution)/shard_map/all_to_all | solution.py:340
  48.5 1.4 shard_map.176
  50.0 8.3 %all-to-all-start.1 = ((f32[16,32,128]{2,1,0:T(8,128)}), f32[16,32,128]{2,1,0:T(8,128)S(1)}, u32[]{:S(2)}, u32[]{:S(2)}) async-start(f32[16,32,128]{2,1,0:T(8,128)} %bitcast.3), calls=%async_computation.1 | async-start | bytes 524288 | tf_op jit(solution)/shard_map/all_to_all | solution.py:340
  58.3 0.0 copy-start.7
  58.3 1.6 %copy-done.7 = f32[4,16,16,512]{3,2,1,0:T(8,128)S(1)} copy-done((f32[4,16,16,512]{3,2,1,0:T(8,128)S(1)}, f32[4,16,16,512]{3,2,1,0:T(8,128)}, u32[]{:S(2)}) %copy-start.7) | copy-done | bytes 2097176
  59.9 14.2 %shard_map.177 = (f32[64,16,512]{2,1,0:T(8,128)S(1)}, f32[64,128]{1,0:T(8,128)S(1)}) custom-call(f32[64,16,512]{2,1,0:T(8,128)S(1)} %copy-done.1, f32[64,16,512]{2,1,0:T(8,128)S(1)} %bitcast.19, f32[64,64]{1,0:T(8,128)S(1)} %copy-done.17), custom_call_target="tpu_custom_call" | custom-call | flops 1073741824 | bytes 6291456 | tf_op jit(solution)/shard_map/pallas_call | solution.py:329
  74.1 1.3 copy-done.4
  75.4 0.6 copy-done.20
  76.0 0.8 copy-done.21
  76.8 0.7 copy-done.23
  77.6 0.7 copy-done.24
  78.3 0.4 shard_map.178
  78.7 11.7 %all_to_all.31 = f32[16,16,128]{2,1,0:T(8,128)S(1)} all-to-all(f32[16,16,128]{2,1,0:T(8,128)S(1)} %bitcast.24), channel_id=1, replica_groups=mesh['px'=16,'py'=16] {'py'}, dimensions={0} | all-to-all | bytes 262144 | tf_op jit(solution)/shard_map/all_to_all | solution.py:340
  90.4 0.7 shard_map.179
  91.2 10.4 %all_to_all.32 = f32[16,4,128]{2,1,0:T(4,128)S(1)} all-to-all(f32[16,4,128]{2,1,0:T(4,128)S(1)} %bitcast.26), channel_id=1, replica_groups=mesh['px'=16,'py'=16] {'py'}, dimensions={0} | all-to-all | bytes 65536 | tf_op jit(solution)/shard_map/all_to_all | solution.py:340
  101.6 0.6 shard_map.180
  102.2 15.0 %all_to_all.33 = f32[16,24,128]{2,1,0:T(8,128)S(1)} all-to-all(f32[16,24,128]{2,1,0:T(8,128)S(1)} %shard_map.180), channel_id=1, replica_groups=mesh['px'=16,'py'=16] {'px'}, dimensions={0} | all-to-all | bytes 393216 | tf_op jit(solution)/shard_map/all_to_all | solution.py:340
  117.2 0.0 copy-start.9
  117.2 1.4 shard_map.181
  118.6 5.6 %all-to-all-start.5 = ((f32[16,128,128]{2,1,0:T(8,128)}), f32[16,128,128]{2,1,0:T(8,128)S(1)}, u32[]{:S(2)}, u32[]{:S(2)}) async-start(f32[16,128,128]{2,1,0:T(8,128)} %shard_map.181), calls=%async_computation.5 | async-start | bytes 2097152 | tf_op jit(solution)/shard_map/all_to_all | solution.py:340
  124.3 1.6 %shard_map.183 = f32[2048,128]{1,0:T(8,128)} custom-call(f32[64,128]{1,0:T(8,128)S(1)} %get-tuple-element.21.xr_ref, f32[64,128]{1,0:T(8,128)S(1)} %copy-done.19, f32[32,128]{1,0:T(8,128)S(1)} %get-tuple-element.23.b1_ref), custom_call_target="tpu_custom_call" | custom-call | flops 1048576 | bytes 1048576 | tf_op jit(solution)/shard_map/pallas_call | solution.py:329
  125.9 15.7 %all-to-all-done.5.in_ref.mixed_ref = f32[16,128,128]{2,1,0:T(8,128)S(1)} async-done(((f32[16,128,128]{2,1,0:T(8,128)}), f32[16,128,128]{2,1,0:T(8,128)S(1)}, u32[]{:S(2)}, u32[]{:S(2)}) %all-to-all-start.5) | async-done | bytes 1048608 | tf_op jit(solution)/shard_map/all_to_all | solution.py:340
  141.6 0.9 copy-done.10
  142.5 4.0 %shard_map.182 = (f32[4,16,16,512]{3,2,1,0:T(8,128)}, f32[64,64]{1,0:T(8,128)}) custom-call(f32[16,128,128]{2,1,0:T(8,128)S(1)} %all-to-all-done.5.in_ref.mixed_ref, f32[16,128,128]{2,1,0:T(8,128)S(1)} %all-to-all-done.5.in_ref.mixed_ref, f32[4,16,16,512]{3,2,1,0:T(8,128)S(1)} %bitcast.18, bf16[256,512]{1,0:T(8,128)(2,1)S(1)} %copy-done.10, ...), custom_call_target="tpu_custom_call" | custom-call | tf_op jit(solution)/shard_map/pallas_call | solution.py:405
  (35 shorter events, 0.1 us)
Async XLA Ops:
  0.6 1.6 %copy-start = (f32[64,16,512]{2,1,0:T(8,128)S(1)}, f32[64,16,512]{2,1,0:T(8,128)}, u32[]{:S(2)}) copy-start(f32[64,16,512]{2,1,0:T(8,128)} %x_ref.1) | copy-start | bytes 6291460
  2.2 1.6 %copy-start.2 = (f32[64,16,512]{2,1,0:T(8,128)S(1)}, f32[64,16,512]{2,1,0:T(8,128)}, u32[]{:S(2)}) copy-start(f32[64,16,512]{2,1,0:T(8,128)} %param.17) | copy-start | bytes 6291460
  3.8 1.6 %copy-start.3 = (f32[64,16,512]{2,1,0:T(8,128)S(1)}, f32[64,16,512]{2,1,0:T(8,128)}, u32[]{:S(2)}) copy-start(f32[64,16,512]{2,1,0:T(8,128)} %param.18) | copy-start | bytes 6291460
  5.4 0.9 copy-start.12
  6.4 0.9 copy-start.13
  11.9 36.6 %copy-start.6 = (f32[4,16,16,512]{3,2,1,0:T(8,128)}, f32[4,16,16,512]{3,2,1,0:T(8,128)S(1)}, u32[]{:S(2)}) copy-start(f32[4,16,16,512]{3,2,1,0:T(8,128)S(1)} %get-tuple-element.15) | copy-start | bytes 6291460
  12.0 36.6 %copy-start.15 = (bf16[64,512]{1,0:T(8,128)(2,1)S(1)}, bf16[64,512]{1,0:T(8,128)(2,1)}, u32[]{:S(2)}) copy-start(bf16[64,512]{1,0:T(8,128)(2,1)} %constant.25.clone.tl_ref) | copy-start | bytes 196612
  12.0 36.5 %copy-start.16 = (bf16[64,512]{1,0:T(8,128)(2,1)S(1)}, bf16[64,512]{1,0:T(8,128)(2,1)}, u32[]{:S(2)}) copy-start(bf16[64,512]{1,0:T(8,128)(2,1)} %constant.24.clone.th_ref) | copy-start | bytes 196612
  48.5 9.8 %copy-start.1 = (f32[64,16,512]{2,1,0:T(8,128)S(1)}, f32[64,16,512]{2,1,0:T(8,128)}, u32[]{:S(2)}) copy-start(f32[64,16,512]{2,1,0:T(8,128)} %x_ref.1) | copy-start | bytes 6291460
  48.5 9.8 %copy-start.17 = (f32[64,64]{1,0:T(8,128)S(1)}, f32[64,64]{1,0:T(8,128)}, u32[]{:S(2)}) copy-start(f32[64,64]{1,0:T(8,128)} %weight_ref.1) | copy-start | bytes 49156
  50.0 26.1 %all-to-all-start.1 = ((f32[16,32,128]{2,1,0:T(8,128)}), f32[16,32,128]{2,1,0:T(8,128)S(1)}, u32[]{:S(2)}, u32[]{:S(2)}) async-start(f32[16,32,128]{2,1,0:T(8,128)} %bitcast.3), calls=%async_computation.1 | async-start | bytes 524288 | tf_op jit(solution)/shard_map/all_to_all | solution.py:340
  58.3 1.6 %copy-start.7 = (f32[4,16,16,512]{3,2,1,0:T(8,128)S(1)}, f32[4,16,16,512]{3,2,1,0:T(8,128)}, u32[]{:S(2)}) copy-start(f32[4,16,16,512]{3,2,1,0:T(8,128)} %copy-done.6) | copy-start | bytes 6291460
  59.9 16.1 %copy-start.22 = (bf16[32,256]{1,0:T(8,128)(2,1)S(1)}, bf16[32,256]{1,0:T(8,128)(2,1)}, u32[]{:S(2)}) copy-start(bf16[32,256]{1,0:T(8,128)(2,1)} %constant.28.clone.bl_ref) | copy-start | bytes 49156
  59.9 30.5 %copy-start.8 = (f32[2,2,8,64,128]{4,3,2,1,0:T(8,128)S(1)}, f32[2,2,8,64,128]{4,3,2,1,0:T(8,128)}, u32[]{:S(2)}) copy-start(f32[2,2,8,64,128]{4,3,2,1,0:T(8,128)} %param.20) | copy-start | bytes 3145732
  59.9 41.7 %copy-start.14 = (bf16[192,256]{1,0:T(8,128)(2,1)S(1)}, bf16[192,256]{1,0:T(8,128)(2,1)}, u32[]{:S(2)}) copy-start(bf16[192,256]{1,0:T(8,128)(2,1)} %constant.29.clone.t_ref) | copy-start | bytes 294916
  74.1 1.3 copy-start.4
  75.4 0.6 copy-start.20
  76.0 41.1 %copy-start.11 = (bf16[512,192]{1,0:T(8,128)(2,1)S(1)}, bf16[512,192]{1,0:T(8,128)(2,1)}, u32[]{:S(2)}) copy-start(bf16[512,192]{1,0:T(8,128)(2,1)} %constant.30.clone.t_ref) | copy-start | bytes 589828
  76.0 0.8 copy-start.21
  76.8 0.7 copy-start.23
  77.6 0.7 copy-start.24
  91.1 26.0 %copy-start.18 = (f32[64,128]{1,0:T(8,128)}, f32[64,128]{1,0:T(8,128)S(1)}, u32[]{:S(2)}) copy-start(f32[64,128]{1,0:T(8,128)S(1)} %get-tuple-element.22.xi_ref) | copy-start | bytes 98308
  117.2 7.1 %copy-start.19 = (f32[64,128]{1,0:T(8,128)S(1)}, f32[64,128]{1,0:T(8,128)}, u32[]{:S(2)}) copy-start(f32[64,128]{1,0:T(8,128)} %copy-done.18) | copy-start | bytes 98308
  117.2 24.4 %copy-start.5 = (f32[64,16,512]{2,1,0:T(8,128)S(1)}, f32[64,16,512]{2,1,0:T(8,128)}, u32[]{:S(2)}) copy-start(f32[64,16,512]{2,1,0:T(8,128)} %copy-done.4) | copy-start | bytes 6291460
  117.2 24.4 %copy-start.9 = (bf16[256,512]{1,0:T(8,128)(2,1)S(1)}, bf16[256,512]{1,0:T(8,128)(2,1)}, u32[]{:S(2)}) copy-start(bf16[256,512]{1,0:T(8,128)(2,1)} %constant.32.clone.dl_ref) | copy-start | bytes 786436
  118.6 22.9 %all-to-all-start.5 = ((f32[16,128,128]{2,1,0:T(8,128)}), f32[16,128,128]{2,1,0:T(8,128)S(1)}, u32[]{:S(2)}, u32[]{:S(2)}) async-start(f32[16,128,128]{2,1,0:T(8,128)} %shard_map.181), calls=%async_computation.5 | async-start | bytes 2097152 | tf_op jit(solution)/shard_map/all_to_all | solution.py:340
  141.5 1.0 copy-start.10
where the time goes:
time: 147 us
  blocking collectives  73.6 us (50%)
  Pallas kernels  29 us (20%)
  waiting for transfers between devices  15.7 us (11%)
  starting transfers between devices  14 us (10%)
  local copies, waits for them, and re-layouts  13.4 us (9%)
    all_to_all x4, blocking collectives, exchange(): return lax.all_to_all(values, axis, split_axis=0, concat_axis=0, tiled=True)  73.6 us
    pallas_call x7, Pallas kernels, call(): pl.pallas_call(body, out_shape=outs, in_specs=whole(len(args)), out_specs...  20.4 us
    all_to_all x2, waiting for transfers between devices, exchange(): return lax.all_to_all(values, axis, split_axis=0, concat_axis=0, tiled=True)  15.7 us
    all_to_all x2, starting transfers between devices, exchange(): return lax.all_to_all(values, axis, split_axis=0, concat_axis=0, tiled=True)  14 us
    unnamed x50, local copies, waits for them, and re-layouts  13.4 us
    pallas_call x1, Pallas kernels, per_device(): pl.pallas_call(start_kernel, grid=(steps,), out_shape=(struct(4, 16, 16,...  4.63 us
    pallas_call x1, Pallas kernels, per_device(): pl.pallas_call(end_kernel, grid=(steps,), out_shape=(struct(4, 16, 16, 51...  4.03 us
  transfers between devices with their start and end apart: 2, of which 1 were waited for; matrix products, arithmetic and copies ran while one was open for 0% of the time, Pallas kernels for 11%

commit v1 on v0

--- a/solution.py
+++ b/solution.py
@@ -24,6 +24,10 @@
     high = table.astype(ml_dtypes.bfloat16)
     low = (table - high.astype(np.float64)).astype(high.dtype)
     return high, low
+
+
+def column(table):
+    return jnp.asarray(np.concatenate(pair(table), axis=0))
 
 
 def frequency(index):
@@ -138,13 +142,13 @@
     return out
 
 
-def start_kernel(x_ref, pre_ref, cot_ref, dh_ref, dl_ref, grad_ref, out_ref):
+def start_kernel(x_ref, pre_ref, cot_ref, table_ref, grad_ref, out_ref):
     v = pre_ref[...]
     cumulative = 0.5 * (1.0 + lax.erf(v * (1.0 / math.sqrt(2.0))))
     density = jnp.exp(-0.5 * v * v) * (1.0 / math.sqrt(2.0 * math.pi))
     grad = cot_ref[...] * (cumulative + v * density)
     grad_ref[...] = grad
-    table = (dh_ref[...], dl_ref[...])
+    table = (table_ref[:256], table_ref[256:])
     for i in range(x_ref.shape[1]):
         rows = jnp.concatenate(
             [x_ref[c, i] for c in range(4)] + [grad[c, i] for c in range(4)], axis=0
@@ -152,39 +156,35 @@
         out_ref[i] = dot3(table, split(rows), ((1,), (1,)))
 
 
-def second_kernel(in_ref, th_ref, tl_ref, out_ref):
-    both = jnp.concatenate([th_ref[...], tl_ref[...]], axis=0)
+def second_kernel(in_ref, table_ref, out_ref):
+    both = table_ref[...]
     for k in range(8):
         rows = jnp.concatenate([in_ref[s, 32 * k : 32 * k + 32, :] for s in range(16)], axis=0)
         high, low = split(rows)
         two = dot(both, high)
-        done = two[:64] + (two[64:] + dot(th_ref[...], low))
+        done = two[:64] + (two[64:] + dot(both[:64], low))
         for ri in range(2):
             for q in range(2):
                 j = 2 * ri + q
                 out_ref[pl.ds(ri * 16 + k * 2 + q, 16, stride=32), :] = done[16 * j : 16 * j + 16]
 
 
-def first_kernel(in_ref, tw_ref, bh_ref, bl_ref, mix_ref, out_ref):
+def first_kernel(in_ref, tw_ref, table_ref, mix_ref, out_ref):
     parts = [(in_ref[32 * s : 32 * s + 16], in_ref[32 * s + 16 : 32 * s + 32]) for s in range(16)]
     rows = []
     for r, (re, im) in enumerate(fft(parts)):
         c, s = tw_ref[r : r + 1], tw_ref[16 + r : 17 + r]
         rows.append(jnp.concatenate([re * c + im * s, im * c - re * s], axis=1))
     data = split(jnp.concatenate(rows, axis=0))
-    done = dot3((bh_ref[...], bl_ref[...]), data, ((1,), (1,)))
-    lane = lanes((16, 128))
+    done = dot3((table_ref[:32], table_ref[32:]), data, ((1,), (1,)))
     for h in range(2):
         for b in range(8):
             tile = done[16 * h : 16 * h + 16, 128 * (b // 4) : 128 * (b // 4) + 128]
             if b % 4:
                 tile = pltpu.roll(tile, 128 - 32 * (b % 4), 1)
             d = 8 * h + b
-            mix = mix_ref[16 * (d // 4) : 16 * (d // 4) + 16]
-            shift = (32 - 16 * (d % 4)) % 128
-            if shift:
-                mix = pltpu.roll(mix, shift, 1)
-            out_ref[16 * d : 16 * d + 16] = jnp.where(lane < 32, tile, mix)
+            out_ref[16 * d : 16 * d + 16] = tile
+            out_ref[16 * d : 16 * d + 4, 64:128] = mix_ref[4 * d : 4 * d + 4, 64:128]
 
 
 def swap_halves(b1):
@@ -218,10 +218,10 @@
     xr_ref[...] = field(0, 0)
     xi_ref[...] = field(1, 0)
     b1_ref[...] = b1
-    mix = in_ref[0:16]
+    mix = in_ref[0:4]
     for s in range(1, 16):
-        mix = mix + in_ref[16 * s : 16 * s + 16]
-    mix_ref[...] = jnp.where(lanes((8, 128)) < 48, mix[:8], pltpu.roll(mix[8:], 16, 1))
+        mix = mix + in_ref[16 * s : 16 * s + 4]
+    mix_ref[...] = jnp.where(lanes((2, 128)) < 64, pltpu.roll(mix, 64, 1)[:2], mix[2:])
 
 
 def outer_kernel(xr_ref, xi_ref, b1_ref, out_ref):
@@ -254,29 +254,30 @@
     for t in range(2):
         blocks = [done[16 * b : 16 * b + 16, 128 * t : 128 * t + 128] for b in range(8)]
         for g, block in enumerate(transpose_groups(blocks, 16)):
-            out_ref[8 * t + g, 0:16, :] = block
-            out_ref[8 * t + g, 16:24, :] = mix
+            at = 18 * (8 * t + g)
+            out_ref[at : at + 16] = block
+            out_ref[at + 16 : at + 18] = mix
 
 
 def second_back_kernel(in_ref, t_ref, out_ref):
     for k in range(4):
         rows = jnp.concatenate(
-            [in_ref[pl.ds(4 * k + j, 16, stride=24), :] for j in range(4)], axis=0
+            [in_ref[pl.ds(4 * k + j, 16, stride=18), :] for j in range(4)], axis=0
         )
         high, low = split(rows)
         done = dot(t_ref[...], jnp.concatenate([high, high, low], axis=0))
         for y in range(16):
             out_ref[y, 32 * k : 32 * k + 32, :] = done[32 * y : 32 * y + 32]
-    mix = in_ref[16:24]
+    mix = in_ref[16:18]
     for s in range(1, 16):
-        mix = mix + in_ref[24 * s + 16 : 24 * s + 24]
-    lane = lanes((8, 128))
+        mix = mix + in_ref[18 * s + 16 : 18 * s + 18]
+    mix = jnp.concatenate([mix, pltpu.roll(mix, 64, 1)], axis=0)
     for y in range(16):
-        out_ref[y, 16:24, :] = jnp.where(lane < 64, mix, out_ref[y, 16:24, :])
-
-
-def end_kernel(in_ref, mixed_ref, direct_ref, dh_ref, dl_ref, out_ref, mix_ref):
-    table = (dh_ref[...], dl_ref[...])
+        out_ref[y, 16:20, 0:64] = mix[:, :64]
+
+
+def end_kernel(in_ref, mixed_ref, direct_ref, table_ref, out_ref, mix_ref):
+    table = (table_ref[:256], table_ref[256:])
     for i in range(in_ref.shape[0]):
         turned = in_ref[i].T
         rows = jnp.concatenate([turned[:64], turned[64:]], axis=1)
@@ -286,18 +287,8 @@
 
     @pl.when(pl.program_id(0) == 0)
     def _():
-        lane = lanes((8, 128))
-        scale = 1.0 / math.sqrt(CELLS)
-        for block in range(4):
-            for half in range(2):
-                total = None
-                for o in range(4):
-                    part = mixed_ref[4 * block + o]
-                    shift = (16 * o - 32 - 16 * half) % 128
-                    part = pltpu.roll(part, shift, 1) if shift else part
-                    total = part if total is None else jnp.where(lane // 16 == o, part, total)
-                at = 16 * block + 8 * half
-                mix_ref[at : at + 8, :] = total[:, :64] * scale
+        for d in range(16):
+            mix_ref[4 * d : 4 * d + 4] = mixed_ref[d, 0:4, 0:64] * (1.0 / math.sqrt(CELLS))
 
 
 def side_kernel(x_ref, grad_ref, weight_ref, direct_ref, mix_ref):
@@ -305,11 +296,20 @@
     weight = jnp.concatenate([high, low, high], axis=1)
     total = jnp.zeros((64, 64), F32)
     for x in range(16):
-        field = split(x_ref[:, x, :])
-        gh, gl = split(grad_ref[:, x, :])
+        field = split(x_ref[pl.ds(x, 64, stride=16), :])
+        gh, gl = split(grad_ref[pl.ds(x, 64, stride=16), :])
         total = total + dot3(field, (gh, gl), ((1,), (1,)))
-        direct_ref[:, x, :] = dot(weight, jnp.concatenate([gh, gh, gl], axis=0))
-    mix_ref[...] = jnp.concatenate([total, total], axis=1)
+        direct_ref[pl.ds(x, 64, stride=16), :] = dot(weight, jnp.concatenate([gh, gh, gl], axis=0))
+    total = jnp.concatenate([total, total], axis=1)
+    first = pl.program_id(0) == 0
+
+    @pl.when(first)
+    def _():
+        mix_ref[...] = total
+
+    @pl.when(jnp.logical_not(first))
+    def _():
+        mix_ref[...] += total
 
 
 def params(mebibytes):
@@ -324,7 +324,7 @@
     return jax.ShapeDtypeStruct(shape, F32)
 
 
-def call(body, outs, args, mebibytes=16, cost=None):
+def call(body, outs, args, mebibytes=12, cost=None):
     many = isinstance(outs, tuple)
     return pl.pallas_call(
         body,
@@ -346,40 +346,43 @@
 
 
 def per_device(inputs, pre_act, cotangent, mix_weight, spectral_weight):
-    steps, per = 4, 4
+    steps, per = 8, 2
     field_spec = pl.BlockSpec((4, per, 16, 512), lambda i: (0, i, 0, 0))
-    table_spec = pl.BlockSpec((256, 512), lambda i: (0, 0))
+    table_spec = pl.BlockSpec((512, 512), lambda i: (0, 0))
     shaped = [a.reshape(4, 16, 16, 512) for a in (inputs, pre_act, cotangent)]
     grad_pre, depth = pl.pallas_call(
         start_kernel,
         grid=(steps,),
         out_shape=(struct(4, 16, 16, 512), struct(16, 256, 128)),
-        in_specs=[field_spec] * 3 + [table_spec] * 2,
+        in_specs=[field_spec] * 3 + [table_spec],
         out_specs=(field_spec, pl.BlockSpec((per, 256, 128), lambda i: (i, 0, 0))),
-        compiler_params=params(32),
-    )(*shaped, *map(jnp.asarray, pair(depth_forward())))
-
-    depth = exchange(depth, "py")
-    direct, mix = call(
+        compiler_params=params(60),
+    )(*shaped, column(depth_forward()))
+
+    tile_spec = pl.BlockSpec((1024, 128), lambda i: (0, i))
+    direct, mix = pl.pallas_call(
         side_kernel,
-        (struct(64, 16, 512), struct(64, 128)),
-        (inputs, grad_pre.reshape(64, 16, 512), mix_weight),
-        24,
-        pl.CostEstimate(flops=1 << 30, bytes_accessed=6 << 20, transcendentals=0),
-    )
+        grid=(4,),
+        out_shape=(struct(1024, 512), struct(64, 128)),
+        in_specs=[tile_spec, tile_spec, pl.BlockSpec((64, 64), lambda i: (0, 0))],
+        out_specs=(tile_spec, pl.BlockSpec((64, 128), lambda i: (0, 0))),
+        compiler_params=params(60),
+        cost_estimate=pl.CostEstimate(flops=1 << 30, bytes_accessed=6 << 20, transcendentals=0),
+    )(inputs.reshape(1024, 512), grad_pre.reshape(1024, 512), mix_weight)
+    depth, direct, mix = lax.optimization_barrier((exchange(depth, "py"), direct, mix))
     along_second = call(
-        second_kernel, struct(512, 128), (depth, *map(jnp.asarray, pair(second_forward()))), 16
+        second_kernel, struct(512, 128), (depth, column(second_forward()))
     )
     along_second = exchange(along_second.reshape(16, 32, 128), "px").reshape(512, 128)
     along_first = call(
         first_kernel,
         struct(256, 128),
-        (along_second, jnp.asarray(first_twiddle()), *map(jnp.asarray, pair(first_halves())), mix),
+        (along_second, jnp.asarray(first_twiddle()), column(first_halves()), mix),
     )
     spectra = exchange(along_first.reshape(16, 16, 128), "py").reshape(256, 128)
     mode_back, xr, xi, b1, mix = call(
         mode_kernel,
-        (struct(64, 128), struct(64, 128), struct(64, 128), struct(32, 128), struct(8, 128)),
+        (struct(64, 128), struct(64, 128), struct(64, 128), struct(32, 128), struct(2, 128)),
         (spectra, spectral_weight.reshape(2048, 128)),
     )
     mode_back = exchange(mode_back.reshape(16, 4, 128), "py").reshape(64, 128)
@@ -387,15 +390,15 @@
         outer_kernel,
         struct(2048, 128),
         (xr, xi, b1),
-        16,
+        8,
         pl.CostEstimate(flops=1 << 20, bytes_accessed=1 << 20, transcendentals=0),
     ).reshape(spectral_weight.shape)
     first_high, first_low = pair(first_inverse())
     first_table = np.concatenate([first_high, first_low, first_high], axis=0)
     first_back = call(
-        first_back_kernel, struct(16, 24, 128), (mode_back, jnp.asarray(first_table), mix)
-    )
-    first_back = exchange(first_back, "px").reshape(384, 128)
+        first_back_kernel, struct(288, 128), (mode_back, jnp.asarray(first_table), mix)
+    )
+    first_back = exchange(first_back.reshape(16, 1, 2304), "px").reshape(288, 128)
     second_back = call(
         second_back_kernel,
         struct(16, 128, 128),
@@ -411,7 +414,6 @@
             pl.BlockSpec((16, 8, 128), lambda i: (0, 2, 0)),
             field_spec,
             table_spec,
-            table_spec,
         ],
         out_specs=(field_spec, pl.BlockSpec((64, 64), lambda i: (0, 0))),
         compiler_params=params(24),
@@ -419,7 +421,7 @@
         gathered,
         gathered,
         direct.reshape(4, 16, 16, 512),
-        *map(jnp.asarray, pair(depth_inverse())),
+        column(depth_inverse()),
     )
     return (input_grad.reshape(inputs.shape), spectral_grad, mix_grad)
 

time: 147 us -> 133 us (0.905)
  waiting for transfers between devices: 15.7 us -> 37.9 us
  blocking collectives: 73.6 us -> 52.1 us
  local copies, waits for them, and re-layouts: 13.4 us -> 1.08 us
  Pallas kernels: 29 us -> 26.3 us
    all_to_all x2, waiting for transfers between devices: 15.7 us -> 37.9 us  [exchange(): return lax.all_to_all(values, axis, split_axis=0, concat_axis=0, tiled=True)]
    all_to_all x4, blocking collectives: 73.6 us -> 52.1 us  [exchange(): return lax.all_to_all(values, axis, split_axis=0, concat_axis=0, tiled=True)]
    pallas_call x7 -> x6, Pallas kernels: 20.4 us -> 5.46 us  [call(): pl.pallas_call(body, out_shape=outs, in_specs=whole(len(args)), out_specs...]
    unnamed x50 -> x18, local copies, waits for them, and re-layouts: 13.4 us -> 1.08 us
    pallas_call x0 -> x1, Pallas kernels: none -> 6.24 us  [per_device(): pl.pallas_call(side_kernel, grid=(4,), out_shape=(struct(1024, 512), stru...]
    pallas_call x1, Pallas kernels: 4.63 us -> 9.38 us  [per_device(): pl.pallas_call(start_kernel, grid=(steps,), out_shape=(struct(4, 16, 16,...]
  transfers between devices with their start and end apart: 2 -> 2, of which waited for: 1 -> 2; matrix products, arithmetic and copies ran while one was open for 0% -> 0% of each run, Pallas kernels for 11% -> 6%
where the time goes in v1:
time: 133 us; the launch traced here: 132 us
  blocking collectives  52.1 us (39%)
  waiting for transfers between devices  37.9 us (28%)
  Pallas kernels  26.3 us (20%)
  starting transfers between devices  13.9 us (10%)
    all_to_all x4, blocking collectives, exchange(): return lax.all_to_all(values, axis, split_axis=0, concat_axis=0, tiled=True)  52.1 us
    all_to_all x2, waiting for transfers between devices, exchange(): return lax.all_to_all(values, axis, split_axis=0, concat_axis=0, tiled=True)  37.9 us
    all_to_all x2, starting transfers between devices, exchange(): return lax.all_to_all(values, axis, split_axis=0, concat_axis=0, tiled=True)  13.9 us
    pallas_call x1, Pallas kernels, per_device(): pl.pallas_call(start_kernel, grid=(steps,), out_shape=(struct(4, 16, 16,...  9.38 us
    pallas_call x1, Pallas kernels, per_device(): pl.pallas_call(side_kernel, grid=(4,), out_shape=(struct(1024, 512), stru...  6.24 us
    pallas_call x6, Pallas kernels, call(): pl.pallas_call(body, out_shape=outs, in_specs=whole(len(args)), out_specs...  5.46 us
    pallas_call x1, Pallas kernels, per_device(): pl.pallas_call(end_kernel, grid=(steps,), out_shape=(struct(4, 16, 16, 51...  5.22 us
  transfers between devices with their start and end apart: 2, of which 2 were waited for; matrix products, arithmetic and copies ran while one was open for 0% of the time, Pallas kernels for 6%

profile of v1, /device:TPU:1, one launch (start us, length us, event | category | flops | bytes accessed | tf_op | source)
XLA Modules:
  0.0 131.9 jit_solution(17811613448678323987)
XLA Ops:
  0.6 9.4 %shard_map.139 = (f32[4,16,16,512]{3,2,1,0:T(8,128)}, f32[16,256,128]{2,1,0:T(8,128)}) custom-call(f32[4,16,16,512]{3,2,1,0:T(8,128)} %bitcast.27, f32[4,16,16,512]{3,2,1,0:T(8,128)} %bitcast.29, f32[4,16,16,512]{3,2,1,0:T(8,128)} %bitcast.30, bf16[512,512]{1,0:T(8,128)(2,1)} %constant.14.clone.table_ref), custom_call_target="tpu_custom_call" | custom-call | tf_op jit(solution)/shard_map/pallas_call | solution.py:353
  10.0 8.5 %all-to-all-start = ((f32[16,256,128]{2,1,0:T(8,128)}), f32[16,256,128]{2,1,0:T(8,128)S(1)}, u32[]{:S(2)}, u32[]{:S(2)}) async-start(f32[16,256,128]{2,1,0:T(8,128)} %get-tuple-element.17), calls=%async_computation | async-start | bytes 4194304 | tf_op jit(solution)/shard_map/all_to_all | solution.py:340
  18.5 0.0 copy-start.4
  18.5 6.2 %shard_map.140 = (f32[1024,512]{1,0:T(8,128)}, f32[64,128]{1,0:T(8,128)}) custom-call(f32[1024,512]{1,0:T(8,128)} %bitcast.28, f32[1024,512]{1,0:T(8,128)} %bitcast.31, f32[64,64]{1,0:T(8,128)} %weight_ref.1), custom_call_target="tpu_custom_call" | custom-call | flops 1073741824 | bytes 6291456 | tf_op jit(solution)/shard_map/pallas_call | solution.py:363
  24.7 0.0 copy-start.6
  24.7 0.0 copy-start.7
  24.7 0.0 copy-start.8
  24.7 0.0 copy-start.1
  24.7 22.2 %all-to-all-done.in_ref = f32[16,256,128]{2,1,0:T(8,128)S(1)} async-done(((f32[16,256,128]{2,1,0:T(8,128)}), f32[16,256,128]{2,1,0:T(8,128)S(1)}, u32[]{:S(2)}, u32[]{:S(2)}) %all-to-all-start) | async-done | bytes 2097184 | tf_op jit(solution)/shard_map/all_to_all | solution.py:340
  46.9 0.0 copy-done.4
  46.9 0.7 shard_map.141
  47.7 0.0 copy-start.3
  47.7 16.4 %all_to_all.30 = f32[16,32,128]{2,1,0:T(8,128)S(1)} all-to-all(f32[16,32,128]{2,1,0:T(8,128)S(1)} %bitcast.18), channel_id=1, replica_groups=mesh['px'=16,'py'=16] {'px'}, dimensions={0} | all-to-all | bytes 524288 | tf_op jit(solution)/shard_map/all_to_all | solution.py:340
  64.0 0.0 copy-done.6
  64.0 0.0 copy-done.7
  64.0 0.0 copy-done.8
  64.1 0.4 shard_map.142
  64.5 14.0 %all_to_all.31 = f32[16,16,128]{2,1,0:T(8,128)S(1)} all-to-all(f32[16,16,128]{2,1,0:T(8,128)S(1)} %bitcast.24), channel_id=1, replica_groups=mesh['px'=16,'py'=16] {'py'}, dimensions={0} | all-to-all | bytes 262144 | tf_op jit(solution)/shard_map/all_to_all | solution.py:340
  78.5 0.0 copy-done.1
  78.5 0.7 shard_map.143
  79.2 10.4 %all_to_all.32 = f32[16,4,128]{2,1,0:T(4,128)S(1)} all-to-all(f32[16,4,128]{2,1,0:T(4,128)S(1)} %bitcast.26), channel_id=1, replica_groups=mesh['px'=16,'py'=16] {'py'}, dimensions={0} | all-to-all | bytes 65536 | tf_op jit(solution)/shard_map/all_to_all | solution.py:340
  89.6 0.0 copy-done.5
  89.6 0.6 shard_map.144
  90.2 11.3 %all_to_all.33 = f32[16,1,2304]{2,1,0:T(1,128)S(1)} all-to-all(f32[16,1,2304]{2,1,0:T(1,128)S(1)} %bitcast.21), channel_id=1, replica_groups=mesh['px'=16,'py'=16] {'px'}, dimensions={0} | all-to-all | bytes 294912 | tf_op jit(solution)/shard_map/all_to_all | solution.py:340
  101.5 0.0 copy-done.3
  101.5 1.4 %shard_map.145 = f32[16,128,128]{2,1,0:T(8,128)} custom-call(f32[288,128]{1,0:T(8,128)S(1)} %bitcast.22, bf16[512,192]{1,0:T(8,128)(2,1)S(1)} %copy-done.3), custom_call_target="tpu_custom_call" | custom-call | tf_op jit(solution)/shard_map/pallas_call | solution.py:329
  102.9 5.5 %all-to-all-start.5 = ((f32[16,128,128]{2,1,0:T(8,128)}), f32[16,128,128]{2,1,0:T(8,128)S(1)}, u32[]{:S(2)}, u32[]{:S(2)}) async-start(f32[16,128,128]{2,1,0:T(8,128)} %shard_map.145), calls=%async_computation.5 | async-start | bytes 2097152 | tf_op jit(solution)/shard_map/all_to_all | solution.py:340
  108.4 1.6 %shard_map.147 = f32[2048,128]{1,0:T(8,128)} custom-call(f32[64,128]{1,0:T(8,128)S(1)} %get-tuple-element.27.xr_ref, f32[64,128]{1,0:T(8,128)S(1)} %get-tuple-element.28.xi_ref, f32[32,128]{1,0:T(8,128)S(1)} %get-tuple-element.29.b1_ref), custom_call_target="tpu_custom_call" | custom-call | flops 1048576 | bytes 1048576 | tf_op jit(solution)/shard_map/pallas_call | solution.py:329
  110.0 15.7 %all-to-all-done.5.in_ref.mixed_ref = f32[16,128,128]{2,1,0:T(8,128)S(1)} async-done(((f32[16,128,128]{2,1,0:T(8,128)}), f32[16,128,128]{2,1,0:T(8,128)S(1)}, u32[]{:S(2)}, u32[]{:S(2)}) %all-to-all-start.5) | async-done | bytes 1048608 | tf_op jit(solution)/shard_map/all_to_all | solution.py:340
  125.6 0.0 copy-done
  125.7 1.0 copy-done.2
  126.7 5.2 %shard_map.146 = (f32[4,16,16,512]{3,2,1,0:T(8,128)}, f32[64,64]{1,0:T(8,128)}) custom-call(f32[16,128,128]{2,1,0:T(8,128)S(1)} %all-to-all-done.5.in_ref.mixed_ref, f32[16,128,128]{2,1,0:T(8,128)S(1)} %all-to-all-done.5.in_ref.mixed_ref, f32[4,16,16,512]{3,2,1,0:T(8,128)S(1)} %bitcast.17, bf16[512,512]{1,0:T(8,128)(2,1)S(1)} %copy-done.2), custom_call_target="tpu_custom_call" | custom-call | tf_op jit(solution)/shard_map/pallas_call | solution.py:408
  (3 shorter events, 0.0 us)
Async XLA Ops:
  10.0 36.9 %all-to-all-start = ((f32[16,256,128]{2,1,0:T(8,128)}), f32[16,256,128]{2,1,0:T(8,128)S(1)}, u32[]{:S(2)}, u32[]{:S(2)}) async-start(f32[16,256,128]{2,1,0:T(8,128)} %get-tuple-element.17), calls=%async_computation | async-start | bytes 4194304 | tf_op jit(solution)/shard_map/all_to_all | solution.py:340
  18.5 28.5 %copy-start.4 = (bf16[128,512]{1,0:T(8,128)(2,1)S(1)}, bf16[128,512]{1,0:T(8,128)(2,1)}, u32[]{:S(2)}) copy-start(bf16[128,512]{1,0:T(8,128)(2,1)} %constant.15.clone.table_ref) | copy-start | bytes 393220
  24.7 39.3 %copy-start.6 = (bf16[64,256]{1,0:T(8,128)(2,1)S(1)}, bf16[64,256]{1,0:T(8,128)(2,1)}, u32[]{:S(2)}) copy-start(bf16[64,256]{1,0:T(8,128)(2,1)} %constant.17.clone.table_ref) | copy-start | bytes 98308
  24.7 39.3 %copy-start.7 = (f32[64,128]{1,0:T(8,128)S(1)}, f32[64,128]{1,0:T(8,128)}, u32[]{:S(2)}) copy-start(f32[64,128]{1,0:T(8,128)} %get-tuple-element.22.mix_ref) | copy-start | bytes 98308
  24.7 39.3 %copy-start.8 = (f32[32,128]{1,0:T(8,128)S(1)}, f32[32,128]{1,0:T(8,128)}, u32[]{:S(2)}) copy-start(f32[32,128]{1,0:T(8,128)} %constant.16.clone.tw_ref) | copy-start | bytes 49156
  24.7 53.7 %copy-start.1 = (f32[2,2,8,64,128]{4,3,2,1,0:T(8,128)S(1)}, f32[2,2,8,64,128]{4,3,2,1,0:T(8,128)}, u32[]{:S(2)}) copy-start(f32[2,2,8,64,128]{4,3,2,1,0:T(8,128)} %param.16) | copy-start | bytes 3145732
  46.9 42.7 %copy-start.5 = (bf16[192,256]{1,0:T(8,128)(2,1)S(1)}, bf16[192,256]{1,0:T(8,128)(2,1)}, u32[]{:S(2)}) copy-start(bf16[192,256]{1,0:T(8,128)(2,1)} %constant.18.clone.t_ref) | copy-start | bytes 294916
  47.7 53.8 %copy-start.3 = (bf16[512,192]{1,0:T(8,128)(2,1)S(1)}, bf16[512,192]{1,0:T(8,128)(2,1)}, u32[]{:S(2)}) copy-start(bf16[512,192]{1,0:T(8,128)(2,1)} %constant.19.clone.t_ref) | copy-start | bytes 589828
  101.5 24.1 %copy-start = (f32[1024,512]{1,0:T(8,128)S(1)}, f32[1024,512]{1,0:T(8,128)}, u32[]{:S(2)}) copy-start(f32[1024,512]{1,0:T(8,128)} %get-tuple-element.25) | copy-start | bytes 6291460
  102.9 22.7 %all-to-all-start.5 = ((f32[16,128,128]{2,1,0:T(8,128)}), f32[16,128,128]{2,1,0:T(8,128)S(1)}, u32[]{:S(2)}, u32[]{:S(2)}) async-start(f32[16,128,128]{2,1,0:T(8,128)} %shard_map.145), calls=%async_computation.5 | async-start | bytes 2097152 | tf_op jit(solution)/shard_map/all_to_all | solution.py:340
  125.7 1.0 copy-start.2

commit v2 on v1

--- a/solution.py
+++ b/solution.py
@@ -16,6 +16,9 @@
 MZ = 8
 CELLS = NX * NY * NZ
 N = 16
+ROWS = 240
+PER = 2
+PARTS = N // PER
 F32 = jnp.float32
 BF16 = jnp.bfloat16
 
@@ -43,6 +46,10 @@
     t = angle(k, z, 32)
     parts = np.stack([np.cos(t), -np.sin(t)], 1)
     return np.einsum("krz,ab->krabz", parts, np.eye(16)).reshape(256, 512)
+
+
+def depth_sent():
+    return np.delete(depth_forward(), np.arange(16, 32), axis=0)
 
 
 def depth_inverse():
@@ -56,6 +63,10 @@
     full = np.stack([np.stack([c, s], 1), np.stack([-s, c], 1)], 0)
     full = full.reshape(2, 16, 2, 2, 16, 16)
     return full.transpose(0, 2, 1, 4, 3, 5).reshape(64, 512)
+
+
+def second_real():
+    return second_forward().reshape(64, 16, 2, 16)[:, :, 0].reshape(64, 256)
 
 
 def second_inverse():
@@ -142,24 +153,49 @@
     return out
 
 
-def start_kernel(x_ref, pre_ref, cot_ref, table_ref, grad_ref, out_ref):
-    v = pre_ref[...]
+def slope(v):
     cumulative = 0.5 * (1.0 + lax.erf(v * (1.0 / math.sqrt(2.0))))
     density = jnp.exp(-0.5 * v * v) * (1.0 / math.sqrt(2.0 * math.pi))
-    grad = cot_ref[...] * (cumulative + v * density)
-    grad_ref[...] = grad
-    table = (table_ref[:256], table_ref[256:])
-    for i in range(x_ref.shape[1]):
-        rows = jnp.concatenate(
-            [x_ref[c, i] for c in range(4)] + [grad[c, i] for c in range(4)], axis=0
-        )
-        out_ref[i] = dot3(table, split(rows), ((1,), (1,)))
-
-
-def second_kernel(in_ref, table_ref, out_ref):
-    both = table_ref[...]
+    return cumulative + v * density
+
+
+def start_kernel(x_hbm, pre_hbm, cot_hbm, table_ref, out_hbm, x, pre, cot, out, in_sems, out_sems):
+    moves = []
+    for i in range(PARTS):
+        at = pl.ds(PER * i, PER)
+        three = [
+            pltpu.make_async_copy(a.at[:, at], b.at[:, at], in_sems.at[n, i])
+            for n, (a, b) in enumerate([(pre_hbm, pre), (cot_hbm, cot), (x_hbm, x)])
+        ]
+        for move in three:
+            move.start()
+        moves.append(three)
+    table = (table_ref[:ROWS], table_ref[ROWS:])
+    sends = []
+    for i in range(PARTS):
+        for move in moves[i]:
+            move.wait()
+        own = slice(PER * i, PER * i + PER)
+        grad = cot[:, own] * slope(pre[:, own])
+        rows = []
+        for j in range(PER):
+            rows += [x[c, PER * i + j] for c in range(4)] + [grad[c, j] for c in range(4)]
+        done = dot3(table, split(jnp.concatenate(rows, axis=0)), ((1,), (1,)))
+        for j in range(PER):
+            out[PER * i + j] = done[:, 128 * j : 128 * j + 128]
+        at = pl.ds(PER * i, PER)
+        send = pltpu.make_async_copy(out.at[at], out_hbm.at[at], out_sems.at[i])
+        send.start()
+        sends.append(send)
+    for send in sends:
+        send.wait()
+
+
+def second_kernel(in_ref, table_ref, real_ref, out_ref):
     for k in range(8):
-        rows = jnp.concatenate([in_ref[s, 32 * k : 32 * k + 32, :] for s in range(16)], axis=0)
+        at, size = (0, 16) if k == 0 else (32 * k - 16, 32)
+        both = real_ref[...] if k == 0 else table_ref[...]
+        rows = jnp.concatenate([in_ref[s, at : at + size, :] for s in range(16)], axis=0)
         high, low = split(rows)
         two = dot(both, high)
         done = two[:64] + (two[64:] + dot(both[:64], low))
@@ -276,28 +312,53 @@
         out_ref[y, 16:20, 0:64] = mix[:, :64]
 
 
-def end_kernel(in_ref, mixed_ref, direct_ref, table_ref, out_ref, mix_ref):
-    table = (table_ref[:256], table_ref[256:])
-    for i in range(in_ref.shape[0]):
-        turned = in_ref[i].T
-        rows = jnp.concatenate([turned[:64], turned[64:]], axis=1)
-        done = dot3(split(rows), table)
-        for c in range(4):
-            out_ref[c, i] = direct_ref[c, i] + done[16 * c : 16 * c + 16]
-
-    @pl.when(pl.program_id(0) == 0)
-    def _():
-        for d in range(16):
-            mix_ref[4 * d : 4 * d + 4] = mixed_ref[d, 0:4, 0:64] * (1.0 / math.sqrt(CELLS))
-
-
-def side_kernel(x_ref, grad_ref, weight_ref, direct_ref, mix_ref):
+def end_kernel(
+    in_ref, direct_hbm, table_hbm, out_hbm, mix_hbm, direct, table, out, mix, sems, in_sems, out_sems
+):
+    table_move = pltpu.make_async_copy(table_hbm, table, sems.at[0])
+    table_move.start()
+    moves = []
+    for i in range(PARTS):
+        at = pl.ds(PER * i, PER)
+        move = pltpu.make_async_copy(direct_hbm.at[:, at], direct.at[:, at], in_sems.at[i])
+        move.start()
+        moves.append(move)
+    for d in range(16):
+        mix[4 * d : 4 * d + 4] = in_ref[d, 16:20, 0:64] * (1.0 / math.sqrt(CELLS))
+    mix_move = pltpu.make_async_copy(mix, mix_hbm, sems.at[1])
+    mix_move.start()
+    sends = []
+    for i in range(PARTS):
+        rows = []
+        for j in range(PER):
+            turned = in_ref[PER * i + j].T
+            rows.append(jnp.concatenate([turned[:64], turned[64:]], axis=1))
+        halves = split(jnp.concatenate(rows, axis=0))
+        if i == 0:
+            table_move.wait()
+        done = dot3(halves, (table[:256], table[256:]))
+        moves[i].wait()
+        for j in range(PER):
+            for c in range(4):
+                at = 64 * j + 16 * c
+                out[c, PER * i + j] = direct[c, PER * i + j] + done[at : at + 16]
+        at = pl.ds(PER * i, PER)
+        send = pltpu.make_async_copy(out.at[:, at], out_hbm.at[:, at], out_sems.at[i])
+        send.start()
+        sends.append(send)
+    for send in sends:
+        send.wait()
+    mix_move.wait()
+
+
+def side_kernel(x_ref, pre_ref, cot_ref, weight_ref, direct_ref, mix_ref):
     high, low = split(weight_ref[...])
     weight = jnp.concatenate([high, low, high], axis=1)
     total = jnp.zeros((64, 64), F32)
     for x in range(16):
         field = split(x_ref[pl.ds(x, 64, stride=16), :])
-        gh, gl = split(grad_ref[pl.ds(x, 64, stride=16), :])
+        at = pl.ds(x, 64, stride=16)
+        gh, gl = split(cot_ref[at, :] * slope(pre_ref[at, :]))
         total = total + dot3(field, (gh, gl), ((1,), (1,)))
         direct_ref[pl.ds(x, 64, stride=16), :] = dot(weight, jnp.concatenate([gh, gh, gl], axis=0))
     total = jnp.concatenate([total, total], axis=1)
@@ -346,32 +407,38 @@
 
 
 def per_device(inputs, pre_act, cotangent, mix_weight, spectral_weight):
-    steps, per = 8, 2
-    field_spec = pl.BlockSpec((4, per, 16, 512), lambda i: (0, i, 0, 0))
-    table_spec = pl.BlockSpec((512, 512), lambda i: (0, 0))
-    shaped = [a.reshape(4, 16, 16, 512) for a in (inputs, pre_act, cotangent)]
-    grad_pre, depth = pl.pallas_call(
+    anywhere = pl.BlockSpec(memory_space=pl.ANY)
+    field = pltpu.VMEM((4, N, N, 512), F32)
+    shaped = [a.reshape(4, N, N, 512) for a in (inputs, pre_act, cotangent)]
+    depth = pl.pallas_call(
         start_kernel,
-        grid=(steps,),
-        out_shape=(struct(4, 16, 16, 512), struct(16, 256, 128)),
-        in_specs=[field_spec] * 3 + [table_spec],
-        out_specs=(field_spec, pl.BlockSpec((per, 256, 128), lambda i: (i, 0, 0))),
+        out_shape=struct(N, ROWS, 128),
+        in_specs=[anywhere] * 3 + whole(1),
+        out_specs=anywhere,
+        scratch_shapes=[
+            field,
+            field,
+            field,
+            pltpu.VMEM((N, ROWS, 128), F32),
+            pltpu.SemaphoreType.DMA((3, PARTS)),
+            pltpu.SemaphoreType.DMA((PARTS,)),
+        ],
         compiler_params=params(60),
-    )(*shaped, column(depth_forward()))
+    )(*shaped, column(depth_sent()))
 
     tile_spec = pl.BlockSpec((1024, 128), lambda i: (0, i))
     direct, mix = pl.pallas_call(
         side_kernel,
         grid=(4,),
         out_shape=(struct(1024, 512), struct(64, 128)),
-        in_specs=[tile_spec, tile_spec, pl.BlockSpec((64, 64), lambda i: (0, 0))],
+        in_specs=[tile_spec] * 3 + [pl.BlockSpec((64, 64), lambda i: (0, 0))],
         out_specs=(tile_spec, pl.BlockSpec((64, 128), lambda i: (0, 0))),
         compiler_params=params(60),
         cost_estimate=pl.CostEstimate(flops=1 << 30, bytes_accessed=6 << 20, transcendentals=0),
-    )(inputs.reshape(1024, 512), grad_pre.reshape(1024, 512), mix_weight)
+    )(*[a.reshape(1024, 512) for a in (inputs, pre_act, cotangent)], mix_weight)
     depth, direct, mix = lax.optimization_barrier((exchange(depth, "py"), direct, mix))
     along_second = call(
-        second_kernel, struct(512, 128), (depth, column(second_forward()))
+        second_kernel, struct(512, 128), (depth, column(second_forward()), column(second_real()))
     )
     along_second = exchange(along_second.reshape(16, 32, 128), "px").reshape(512, 128)
     along_first = call(
@@ -407,22 +474,20 @@
     gathered = exchange(second_back, "py")
     input_grad, mix_grad = pl.pallas_call(
         end_kernel,
-        grid=(steps,),
-        out_shape=(struct(4, 16, 16, 512), struct(64, 64)),
-        in_specs=[
-            pl.BlockSpec((per, 128, 128), lambda i: (i, 0, 0)),
-            pl.BlockSpec((16, 8, 128), lambda i: (0, 2, 0)),
-            field_spec,
-            table_spec,
+        out_shape=(struct(4, N, N, 512), struct(C, C)),
+        in_specs=whole(1) + [anywhere] * 2,
+        out_specs=(anywhere, anywhere),
+        scratch_shapes=[
+            field,
+            pltpu.VMEM((512, 512), BF16),
+            field,
+            pltpu.VMEM((C, C), F32),
+            pltpu.SemaphoreType.DMA((2,)),
+            pltpu.SemaphoreType.DMA((PARTS,)),
+            pltpu.SemaphoreType.DMA((PARTS,)),
         ],
-        out_specs=(field_spec, pl.BlockSpec((64, 64), lambda i: (0, 0))),
-        compiler_params=params(24),
-    )(
-        gathered,
-        gathered,
-        direct.reshape(4, 16, 16, 512),
-        column(depth_inverse()),
-    )
+        compiler_params=params(20),
+    )(gathered, direct.reshape(4, N, N, 512), column(depth_inverse()))
     return (input_grad.reshape(inputs.shape), spectral_grad, mix_grad)
 
 

time: 133 us -> 128 us (0.962)
  waiting for transfers between devices: 37.9 us -> 35.6 us
  Pallas kernels: 26.3 us -> 24.2 us
    pallas_call x2, Pallas kernels: 14.6 us -> 11.7 us  [the longest x1 7.91 us: per_device(): pl.pallas_call(start_kernel, out_shape=struct(N, ROWS, 128), in_specs=[an...]
    all_to_all x2, waiting for transfers between devices: 37.9 us -> 35.6 us  [exchange(): return lax.all_to_all(values, axis, split_axis=0, concat_axis=0, tiled=True)]
  transfers between devices with their start and end apart: 2 -> 2, of which waited for: 2 -> 2; matrix products, arithmetic and copies ran while one was open for 0% -> 0% of each run, Pallas kernels for 6% -> 7%
where the time goes in v2:
time: 128 us
  blocking collectives  52.1 us (41%)
  waiting for transfers between devices  35.6 us (28%)
  Pallas kernels  24.2 us (19%)
  starting transfers between devices  13.9 us (11%)
    all_to_all x4, blocking collectives, exchange(): return lax.all_to_all(values, axis, split_axis=0, concat_axis=0, tiled=True)  52.1 us
    all_to_all x2, waiting for transfers between devices, exchange(): return lax.all_to_all(values, axis, split_axis=0, concat_axis=0, tiled=True)  35.6 us
    all_to_all x2, starting transfers between devices, exchange(): return lax.all_to_all(values, axis, split_axis=0, concat_axis=0, tiled=True)  13.9 us
    pallas_call x1, Pallas kernels, per_device(): pl.pallas_call(start_kernel, out_shape=struct(N, ROWS, 128), in_specs=[an...  7.91 us
    pallas_call x1, Pallas kernels, per_device(): pl.pallas_call(side_kernel, grid=(4,), out_shape=(struct(1024, 512), stru...  7.09 us
    pallas_call x6, Pallas kernels, call(): pl.pallas_call(body, out_shape=outs, in_specs=whole(len(args)), out_specs...  5.43 us
    pallas_call x1, Pallas kernels, per_device(): pl.pallas_call(end_kernel, out_shape=(struct(4, N, N, 512), struct(C, C))...  3.79 us
  transfers between devices with their start and end apart: 2, of which 2 were waited for; matrix products, arithmetic and copies ran while one was open for 0% of the time, Pallas kernels for 7%

profile of v2, /device:TPU:1, one launch (start us, length us, event | category | flops | bytes accessed | tf_op | source)
XLA Modules:
  0.0 127.6 jit_solution(11733332561842486093)
XLA Ops:
  0.6 7.9 %shard_map.148 = f32[16,240,128]{2,1,0:T(8,128)} custom-call(f32[4,16,16,512]{3,2,1,0:T(8,128)} %bitcast.28, f32[4,16,16,512]{3,2,1,0:T(8,128)} %bitcast.30, f32[4,16,16,512]{3,2,1,0:T(8,128)} %bitcast.32, bf16[480,512]{1,0:T(8,128)(2,1)} %constant.16.clone.table_ref), custom_call_target="tpu_custom_call" | custom-call | tf_op jit(solution)/shard_map/pallas_call | solution.py:413
  8.5 8.5 %all-to-all-start = ((f32[16,240,128]{2,1,0:T(8,128)}), f32[16,240,128]{2,1,0:T(8,128)S(1)}, u32[]{:S(2)}, u32[]{:S(2)}) async-start(f32[16,240,128]{2,1,0:T(8,128)} %shard_map.148), calls=%async_computation | async-start | bytes 3932160 | tf_op jit(solution)/shard_map/all_to_all | solution.py:401
  17.0 0.0 copy-start.4
  17.0 0.0 copy-start.6
  17.0 7.1 %shard_map.149 = (f32[1024,512]{1,0:T(8,128)}, f32[64,128]{1,0:T(8,128)}) custom-call(f32[1024,512]{1,0:T(8,128)} %bitcast.29, f32[1024,512]{1,0:T(8,128)} %bitcast.31, f32[1024,512]{1,0:T(8,128)} %bitcast.33, f32[64,64]{1,0:T(8,128)} %weight_ref.1), custom_call_target="tpu_custom_call" | custom-call | flops 1073741824 | bytes 6291456 | tf_op jit(solution)/shard_map/pallas_call | solution.py:430
  24.1 0.0 copy-start.9
  24.1 0.0 copy-start.1
  24.1 19.9 %all-to-all-done.in_ref = f32[16,240,128]{2,1,0:T(8,128)S(1)} async-done(((f32[16,240,128]{2,1,0:T(8,128)}), f32[16,240,128]{2,1,0:T(8,128)S(1)}, u32[]{:S(2)}, u32[]{:S(2)}) %all-to-all-start) | async-done | bytes 1966112 | tf_op jit(solution)/shard_map/all_to_all | solution.py:401
  44.1 0.0 copy-done.4
  44.1 0.0 copy-done.6
  44.1 0.7 shard_map.150
  44.8 0.0 copy-start.3
  44.8 16.3 %all_to_all.30 = f32[16,32,128]{2,1,0:T(8,128)S(1)} all-to-all(f32[16,32,128]{2,1,0:T(8,128)S(1)} %bitcast.19), channel_id=1, replica_groups=mesh['px'=16,'py'=16] {'px'}, dimensions={0} | all-to-all | bytes 524288 | tf_op jit(solution)/shard_map/all_to_all | solution.py:401
  61.1 0.0 copy-done.7
  61.1 0.0 copy-done.8
  61.1 0.0 copy-done.9
  61.1 0.4 shard_map.151
  61.5 14.1 %all_to_all.31 = f32[16,16,128]{2,1,0:T(8,128)S(1)} all-to-all(f32[16,16,128]{2,1,0:T(8,128)S(1)} %bitcast.25), channel_id=1, replica_groups=mesh['px'=16,'py'=16] {'py'}, dimensions={0} | all-to-all | bytes 262144 | tf_op jit(solution)/shard_map/all_to_all | solution.py:401
  75.6 0.0 copy-done.1
  75.6 0.7 shard_map.152
  76.3 10.4 %all_to_all.32 = f32[16,4,128]{2,1,0:T(4,128)S(1)} all-to-all(f32[16,4,128]{2,1,0:T(4,128)S(1)} %bitcast.27), channel_id=1, replica_groups=mesh['px'=16,'py'=16] {'py'}, dimensions={0} | all-to-all | bytes 65536 | tf_op jit(solution)/shard_map/all_to_all | solution.py:401
  86.7 0.0 copy-done.5
  86.7 0.6 shard_map.153
  87.3 11.3 %all_to_all.33 = f32[16,1,2304]{2,1,0:T(1,128)S(1)} all-to-all(f32[16,1,2304]{2,1,0:T(1,128)S(1)} %bitcast.22), channel_id=1, replica_groups=mesh['px'=16,'py'=16] {'px'}, dimensions={0} | all-to-all | bytes 294912 | tf_op jit(solution)/shard_map/all_to_all | solution.py:401
  98.6 0.0 copy-done.3
  98.6 1.4 %shard_map.154 = f32[16,128,128]{2,1,0:T(8,128)} custom-call(f32[288,128]{1,0:T(8,128)S(1)} %bitcast.23, bf16[512,192]{1,0:T(8,128)(2,1)S(1)} %copy-done.3), custom_call_target="tpu_custom_call" | custom-call | tf_op jit(solution)/shard_map/pallas_call | solution.py:390
  100.0 5.4 %all-to-all-start.5 = ((f32[16,128,128]{2,1,0:T(8,128)}), f32[16,128,128]{2,1,0:T(8,128)S(1)}, u32[]{:S(2)}, u32[]{:S(2)}) async-start(f32[16,128,128]{2,1,0:T(8,128)} %shard_map.154), calls=%async_computation.5 | async-start | bytes 2097152 | tf_op jit(solution)/shard_map/all_to_all | solution.py:401
  105.5 1.6 %shard_map.156 = f32[2048,128]{1,0:T(8,128)} custom-call(f32[64,128]{1,0:T(8,128)S(1)} %get-tuple-element.23.xr_ref, f32[64,128]{1,0:T(8,128)S(1)} %get-tuple-element.24.xi_ref, f32[32,128]{1,0:T(8,128)S(1)} %get-tuple-element.25.b1_ref), custom_call_target="tpu_custom_call" | custom-call | flops 1048576 | bytes 1048576 | tf_op jit(solution)/shard_map/pallas_call | solution.py:390
  107.1 15.7 %all-to-all-done.5.in_ref = f32[16,128,128]{2,1,0:T(8,128)S(1)} async-done(((f32[16,128,128]{2,1,0:T(8,128)}), f32[16,128,128]{2,1,0:T(8,128)S(1)}, u32[]{:S(2)}, u32[]{:S(2)}) %all-to-all-start.5) | async-done | bytes 1048608 | tf_op jit(solution)/shard_map/all_to_all | solution.py:401
  122.8 0.0 copy-done
  122.8 1.0 copy-done.2
  123.8 3.8 %shard_map.155 = (f32[4,16,16,512]{3,2,1,0:T(8,128)}, f32[64,64]{1,0:T(8,128)}) custom-call(f32[16,128,128]{2,1,0:T(8,128)S(1)} %all-to-all-done.5.in_ref, f32[4,16,16,512]{3,2,1,0:T(8,128)S(1)} %bitcast.18, bf16[512,512]{1,0:T(8,128)(2,1)S(1)} %copy-done.2), custom_call_target="tpu_custom_call" | custom-call | tf_op jit(solution)/shard_map/pallas_call | solution.py:475
  (5 shorter events, 0.0 us)
Async XLA Ops:
  8.5 35.5 %all-to-all-start = ((f32[16,240,128]{2,1,0:T(8,128)}), f32[16,240,128]{2,1,0:T(8,128)S(1)}, u32[]{:S(2)}, u32[]{:S(2)}) async-start(f32[16,240,128]{2,1,0:T(8,128)} %shard_map.148), calls=%async_computation | async-start | bytes 3932160 | tf_op jit(solution)/shard_map/all_to_all | solution.py:401
  17.0 27.1 %copy-start.4 = (bf16[128,512]{1,0:T(8,128)(2,1)S(1)}, bf16[128,512]{1,0:T(8,128)(2,1)}, u32[]{:S(2)}) copy-start(bf16[128,512]{1,0:T(8,128)(2,1)} %constant.17.clone.table_ref) | copy-start | bytes 393220
  17.0 27.1 %copy-start.6 = (bf16[128,256]{1,0:T(8,128)(2,1)S(1)}, bf16[128,256]{1,0:T(8,128)(2,1)}, u32[]{:S(2)}) copy-start(bf16[128,256]{1,0:T(8,128)(2,1)} %constant.18.clone.real_ref) | copy-start | bytes 196612
  24.1 37.0 %copy-start.7 = (bf16[64,256]{1,0:T(8,128)(2,1)S(1)}, bf16[64,256]{1,0:T(8,128)(2,1)}, u32[]{:S(2)}) copy-start(bf16[64,256]{1,0:T(8,128)(2,1)} %constant.20.clone.table_ref) | copy-start | bytes 98308
  24.1 37.0 %copy-start.8 = (f32[64,128]{1,0:T(8,128)S(1)}, f32[64,128]{1,0:T(8,128)}, u32[]{:S(2)}) copy-start(f32[64,128]{1,0:T(8,128)} %get-tuple-element.18.mix_ref) | copy-start | bytes 98308
  24.1 37.0 %copy-start.9 = (f32[32,128]{1,0:T(8,128)S(1)}, f32[32,128]{1,0:T(8,128)}, u32[]{:S(2)}) copy-start(f32[32,128]{1,0:T(8,128)} %constant.19.clone.tw_ref) | copy-start | bytes 49156
  24.1 51.4 %copy-start.1 = (f32[2,2,8,64,128]{4,3,2,1,0:T(8,128)S(1)}, f32[2,2,8,64,128]{4,3,2,1,0:T(8,128)}, u32[]{:S(2)}) copy-start(f32[2,2,8,64,128]{4,3,2,1,0:T(8,128)} %param.17) | copy-start | bytes 3145732
  44.1 42.7 %copy-start.5 = (bf16[192,256]{1,0:T(8,128)(2,1)S(1)}, bf16[192,256]{1,0:T(8,128)(2,1)}, u32[]{:S(2)}) copy-start(bf16[192,256]{1,0:T(8,128)(2,1)} %constant.21.clone.t_ref) | copy-start | bytes 294916
  44.8 53.8 %copy-start.3 = (bf16[512,192]{1,0:T(8,128)(2,1)S(1)}, bf16[512,192]{1,0:T(8,128)(2,1)}, u32[]{:S(2)}) copy-start(bf16[512,192]{1,0:T(8,128)(2,1)} %constant.22.clone.t_ref) | copy-start | bytes 589828
  98.6 24.2 %copy-start = (f32[1024,512]{1,0:T(8,128)S(1)}, f32[1024,512]{1,0:T(8,128)}, u32[]{:S(2)}) copy-start(f32[1024,512]{1,0:T(8,128)} %get-tuple-element.21) | copy-start | bytes 6291460
  100.0 22.7 %all-to-all-start.5 = ((f32[16,128,128]{2,1,0:T(8,128)}), f32[16,128,128]{2,1,0:T(8,128)S(1)}, u32[]{:S(2)}, u32[]{:S(2)}) async-start(f32[16,128,128]{2,1,0:T(8,128)} %shard_map.154), calls=%async_computation.5 | async-start | bytes 2097152 | tf_op jit(solution)/shard_map/all_to_all | solution.py:401
  122.8 1.0 copy-start.2

commit v3 on v2

--- a/solution.py
+++ b/solution.py
@@ -17,7 +17,8 @@
 CELLS = NX * NY * NZ
 N = 16
 ROWS = 240
-PER = 2
+HALF = ROWS // 2
+PER = 4
 PARTS = N // PER
 F32 = jnp.float32
 BF16 = jnp.bfloat16
@@ -41,19 +42,19 @@
     return 2.0 * np.pi / length * np.mod(a * b, length)
 
 
-def depth_forward():
+def depth_parts(cells):
     k, z = np.arange(8)[:, None], np.arange(32)[None, :]
     t = angle(k, z, 32)
     parts = np.stack([np.cos(t), -np.sin(t)], 1)
-    return np.einsum("krz,ab->krabz", parts, np.eye(16)).reshape(256, 512)
+    return np.einsum("krz,ab->krabz", parts, np.eye(cells)).reshape(8, 2, cells, cells * 32)
 
 
 def depth_sent():
-    return np.delete(depth_forward(), np.arange(16, 32), axis=0)
+    return np.delete(depth_parts(8).reshape(128, 256), np.arange(8, 16), axis=0)
 
 
 def depth_inverse():
-    return depth_forward().reshape(4, 2, 2, 16, 512).transpose(1, 0, 2, 3, 4).reshape(256, 512)
+    return depth_parts(8).reshape(4, 2, 16, 256).transpose(1, 0, 2, 3).reshape(128, 256)
 
 
 def second_forward():
@@ -61,12 +62,12 @@
     t = angle(frequency(q)[:, None], np.arange(256)[None, :], 256)
     c, s = np.cos(t), np.sin(t)
     full = np.stack([np.stack([c, s], 1), np.stack([-s, c], 1)], 0)
-    full = full.reshape(2, 16, 2, 2, 16, 16)
-    return full.transpose(0, 2, 1, 4, 3, 5).reshape(64, 512)
+    full = full.reshape(2, 16, 2, 2, 16, 2, 8)
+    return full.transpose(0, 2, 1, 4, 5, 3, 6).reshape(64, 512)
 
 
 def second_real():
-    return second_forward().reshape(64, 16, 2, 16)[:, :, 0].reshape(64, 256)
+    return second_forward().reshape(64, 32, 2, 8)[:, :, 0].reshape(64, 256)
 
 
 def second_inverse():
@@ -74,8 +75,8 @@
     t = angle(frequency(q)[:, None], np.arange(256)[None, :], 256)
     c, s = np.cos(t), np.sin(t)
     full = np.stack([np.stack([c, s], 0), np.stack([-s, c], 0)], 0)
-    full = full.reshape(2, 2, 16, 2, 16, 16)
-    return full.transpose(4, 1, 5, 0, 3, 2).reshape(512, 64)
+    full = full.reshape(2, 2, 16, 2, 16, 2, 8)
+    return full.transpose(4, 5, 1, 6, 0, 3, 2).reshape(512, 64)
 
 
 def first_twiddle():
@@ -170,19 +171,25 @@
         for move in three:
             move.start()
         moves.append(three)
-    table = (table_ref[:ROWS], table_ref[ROWS:])
+    both = table_ref[...]
     sends = []
     for i in range(PARTS):
         for move in moves[i]:
             move.wait()
         own = slice(PER * i, PER * i + PER)
         grad = cot[:, own] * slope(pre[:, own])
-        rows = []
-        for j in range(PER):
-            rows += [x[c, PER * i + j] for c in range(4)] + [grad[c, j] for c in range(4)]
-        done = dot3(table, split(jnp.concatenate(rows, axis=0)), ((1,), (1,)))
-        for j in range(PER):
-            out[PER * i + j] = done[:, 128 * j : 128 * j + 128]
+        for j in range(0, PER, 2):
+            rows = []
+            for n in (j, j + 1):
+                rows += [x[c, PER * i + n] for c in range(4)] + [grad[c, n] for c in range(4)]
+            rows = jnp.concatenate(rows, axis=0)
+            for half in range(2):
+                high, low = split(rows[:, 256 * half : 256 * half + 256])
+                two = dot(both, high, ((1,), (1,)))
+                done = two[:HALF] + (two[HALF:] + dot(both[:HALF], low, ((1,), (1,))))
+                for n in range(2):
+                    at = slice(HALF * half, HALF * half + HALF)
+                    out[PER * i + j + n, at] = done[:, 128 * n : 128 * n + 128]
         at = pl.ds(PER * i, PER)
         send = pltpu.make_async_copy(out.at[at], out_hbm.at[at], out_sems.at[i])
         send.start()
@@ -193,9 +200,10 @@
 
 def second_kernel(in_ref, table_ref, real_ref, out_ref):
     for k in range(8):
-        at, size = (0, 16) if k == 0 else (32 * k - 16, 32)
+        at, size = (0, 8) if k == 0 else (16 * k - 8, 16)
         both = real_ref[...] if k == 0 else table_ref[...]
-        rows = jnp.concatenate([in_ref[s, at : at + size, :] for s in range(16)], axis=0)
+        pieces = [(s, at + HALF * half) for s in range(16) for half in range(2)]
+        rows = jnp.concatenate([in_ref[s, a : a + size, :] for s, a in pieces], axis=0)
         high, low = split(rows)
         two = dot(both, high)
         done = two[:64] + (two[64:] + dot(both[:64], low))
@@ -303,13 +311,15 @@
         high, low = split(rows)
         done = dot(t_ref[...], jnp.concatenate([high, high, low], axis=0))
         for y in range(16):
-            out_ref[y, 32 * k : 32 * k + 32, :] = done[32 * y : 32 * y + 32]
+            for half in range(2):
+                at, place = 32 * y + 16 * half, 64 * half + 16 * k
+                out_ref[y, place : place + 16, :] = done[at : at + 16]
     mix = in_ref[16:18]
     for s in range(1, 16):
         mix = mix + in_ref[18 * s + 16 : 18 * s + 18]
     mix = jnp.concatenate([mix, pltpu.roll(mix, 64, 1)], axis=0)
     for y in range(16):
-        out_ref[y, 16:20, 0:64] = mix[:, :64]
+        out_ref[y, 8:12, 0:64] = mix[:, :64]
 
 
 def end_kernel(
@@ -324,19 +334,26 @@
         move.start()
         moves.append(move)
     for d in range(16):
-        mix[4 * d : 4 * d + 4] = in_ref[d, 16:20, 0:64] * (1.0 / math.sqrt(CELLS))
+        mix[4 * d : 4 * d + 4] = in_ref[d, 8:12, 0:64] * (1.0 / math.sqrt(CELLS))
     mix_move = pltpu.make_async_copy(mix, mix_hbm, sems.at[1])
     mix_move.start()
     sends = []
     for i in range(PARTS):
-        rows = []
+        rows = [[], []]
         for j in range(PER):
             turned = in_ref[PER * i + j].T
-            rows.append(jnp.concatenate([turned[:64], turned[64:]], axis=1))
-        halves = split(jnp.concatenate(rows, axis=0))
+            for half in range(2):
+                at = slice(64 * half, 64 * half + 64)
+                rows[half].append(jnp.concatenate([turned[:64, at], turned[64:, at]], axis=1))
         if i == 0:
             table_move.wait()
-        done = dot3(halves, (table[:256], table[256:]))
+        parts = []
+        for half in range(2):
+            high, low = split(jnp.concatenate(rows[half], axis=0))
+            parts.append(
+                dot(jnp.concatenate([high, high], axis=1), table[...]) + dot(low, table[:128])
+            )
+        done = jnp.concatenate(parts, axis=1)
         moves[i].wait()
         for j in range(PER):
             for c in range(4):
@@ -407,7 +424,7 @@
 
 
 def per_device(inputs, pre_act, cotangent, mix_weight, spectral_weight):
-    anywhere = pl.BlockSpec(memory_space=pl.ANY)
+    anywhere = pl.BlockSpec(memory_space=pltpu.HBM)
     field = pltpu.VMEM((4, N, N, 512), F32)
     shaped = [a.reshape(4, N, N, 512) for a in (inputs, pre_act, cotangent)]
     depth = pl.pallas_call(
@@ -479,7 +496,7 @@
         out_specs=(anywhere, anywhere),
         scratch_shapes=[
             field,
-            pltpu.VMEM((512, 512), BF16),
+            pltpu.VMEM((256, 256), BF16),
             field,
             pltpu.VMEM((C, C), F32),
             pltpu.SemaphoreType.DMA((2,)),

time: 128 us -> 124 us (0.969)
  Pallas kernels: 24.2 us -> 21.3 us
    pallas_call x1, Pallas kernels: 7.91 us -> 5.36 us  [per_device(): pl.pallas_call(start_kernel, out_shape=struct(N, ROWS, 128), in_specs=[an...]
where the time goes in v3:
time: 124 us
  blocking collectives  52.1 us (42%)
  waiting for transfers between devices  35.6 us (29%)
  Pallas kernels  21.3 us (17%)
  starting transfers between devices  13.9 us (11%)
    all_to_all x4, blocking collectives, exchange(): return lax.all_to_all(values, axis, split_axis=0, concat_axis=0, tiled=True)  52.1 us
    all_to_all x2, waiting for transfers between devices, exchange(): return lax.all_to_all(values, axis, split_axis=0, concat_axis=0, tiled=True)  35.6 us
    all_to_all x2, starting transfers between devices, exchange(): return lax.all_to_all(values, axis, split_axis=0, concat_axis=0, tiled=True)  13.9 us
    pallas_call x1, Pallas kernels, per_device(): pl.pallas_call(side_kernel, grid=(4,), out_shape=(struct(1024, 512), stru...  7.09 us
    pallas_call x6, Pallas kernels, call(): pl.pallas_call(body, out_shape=outs, in_specs=whole(len(args)), out_specs...  5.44 us
    pallas_call x1, Pallas kernels, per_device(): pl.pallas_call(start_kernel, out_shape=struct(N, ROWS, 128), in_specs=[an...  5.36 us
    pallas_call x1, Pallas kernels, per_device(): pl.pallas_call(end_kernel, out_shape=(struct(4, N, N, 512), struct(C, C))...  3.4 us
  transfers between devices with their start and end apart: 2, of which 2 were waited for; matrix products, arithmetic and copies ran while one was open for 0% of the time, Pallas kernels for 7%

profile of v3, /device:TPU:1, one launch (start us, length us, event | category | flops | bytes accessed | tf_op | source)
XLA Modules:
  0.0 123.6 jit_solution(13816286613336696309)
XLA Ops:
  0.6 5.4 %shard_map.148 = f32[16,240,128]{2,1,0:T(8,128)} custom-call(f32[4,16,16,512]{3,2,1,0:T(8,128)} %bitcast.28, f32[4,16,16,512]{3,2,1,0:T(8,128)} %bitcast.30, f32[4,16,16,512]{3,2,1,0:T(8,128)} %bitcast.32, bf16[240,256]{1,0:T(8,128)(2,1)} %constant.16.clone.table_ref), custom_call_target="tpu_custom_call" | custom-call | tf_op jit(solution)/shard_map/pallas_call | solution.py:430
  6.0 8.5 %all-to-all-start = ((f32[16,240,128]{2,1,0:T(8,128)}), f32[16,240,128]{2,1,0:T(8,128)S(1)}, u32[]{:S(2)}, u32[]{:S(2)}) async-start(f32[16,240,128]{2,1,0:T(8,128)} %shard_map.148), calls=%async_computation | async-start | bytes 3932160 | tf_op jit(solution)/shard_map/all_to_all | solution.py:418
  14.5 0.0 copy-start.4
  14.5 0.0 copy-start.6
  14.5 7.1 %shard_map.149 = (f32[1024,512]{1,0:T(8,128)}, f32[64,128]{1,0:T(8,128)}) custom-call(f32[1024,512]{1,0:T(8,128)} %bitcast.29, f32[1024,512]{1,0:T(8,128)} %bitcast.31, f32[1024,512]{1,0:T(8,128)} %bitcast.33, f32[64,64]{1,0:T(8,128)} %weight_ref.1), custom_call_target="tpu_custom_call" | custom-call | flops 1073741824 | bytes 6291456 | tf_op jit(solution)/shard_map/pallas_call | solution.py:447
  21.6 0.0 copy-start.9
  21.6 0.0 copy-start.1
  21.6 19.9 %all-to-all-done.in_ref = f32[16,240,128]{2,1,0:T(8,128)S(1)} async-done(((f32[16,240,128]{2,1,0:T(8,128)}), f32[16,240,128]{2,1,0:T(8,128)S(1)}, u32[]{:S(2)}, u32[]{:S(2)}) %all-to-all-start) | async-done | bytes 1966112 | tf_op jit(solution)/shard_map/all_to_all | solution.py:418
  41.5 0.0 copy-done.4
  41.5 0.0 copy-done.6
  41.5 0.7 shard_map.150
  42.2 0.0 copy-start.2
  42.2 16.3 %all_to_all.30 = f32[16,32,128]{2,1,0:T(8,128)S(1)} all-to-all(f32[16,32,128]{2,1,0:T(8,128)S(1)} %bitcast.19), channel_id=1, replica_groups=mesh['px'=16,'py'=16] {'px'}, dimensions={0} | all-to-all | bytes 524288 | tf_op jit(solution)/shard_map/all_to_all | solution.py:418
  58.6 0.0 copy-done.7
  58.6 0.0 copy-done.8
  58.6 0.0 copy-done.9
  58.6 0.4 shard_map.151
  59.0 14.1 %all_to_all.31 = f32[16,16,128]{2,1,0:T(8,128)S(1)} all-to-all(f32[16,16,128]{2,1,0:T(8,128)S(1)} %bitcast.25), channel_id=1, replica_groups=mesh['px'=16,'py'=16] {'py'}, dimensions={0} | all-to-all | bytes 262144 | tf_op jit(solution)/shard_map/all_to_all | solution.py:418
  73.0 0.0 copy-done.1
  73.0 0.7 shard_map.152
  73.8 10.4 %all_to_all.32 = f32[16,4,128]{2,1,0:T(4,128)S(1)} all-to-all(f32[16,4,128]{2,1,0:T(4,128)S(1)} %bitcast.27), channel_id=1, replica_groups=mesh['px'=16,'py'=16] {'py'}, dimensions={0} | all-to-all | bytes 65536 | tf_op jit(solution)/shard_map/all_to_all | solution.py:418
  84.2 0.0 copy-done.5
  84.2 0.6 shard_map.153
  84.8 11.3 %all_to_all.33 = f32[16,1,2304]{2,1,0:T(1,128)S(1)} all-to-all(f32[16,1,2304]{2,1,0:T(1,128)S(1)} %bitcast.22), channel_id=1, replica_groups=mesh['px'=16,'py'=16] {'px'}, dimensions={0} | all-to-all | bytes 294912 | tf_op jit(solution)/shard_map/all_to_all | solution.py:418
  96.1 0.0 copy-done.2
  96.1 1.4 %shard_map.154 = f32[16,128,128]{2,1,0:T(8,128)} custom-call(f32[288,128]{1,0:T(8,128)S(1)} %bitcast.23, bf16[512,192]{1,0:T(8,128)(2,1)S(1)} %copy-done.2), custom_call_target="tpu_custom_call" | custom-call | tf_op jit(solution)/shard_map/pallas_call | solution.py:407
  97.5 5.4 %all-to-all-start.5 = ((f32[16,128,128]{2,1,0:T(8,128)}), f32[16,128,128]{2,1,0:T(8,128)S(1)}, u32[]{:S(2)}, u32[]{:S(2)}) async-start(f32[16,128,128]{2,1,0:T(8,128)} %shard_map.154), calls=%async_computation.5 | async-start | bytes 2097152 | tf_op jit(solution)/shard_map/all_to_all | solution.py:418
  102.9 1.6 %shard_map.156 = f32[2048,128]{1,0:T(8,128)} custom-call(f32[64,128]{1,0:T(8,128)S(1)} %get-tuple-element.23.xr_ref, f32[64,128]{1,0:T(8,128)S(1)} %get-tuple-element.24.xi_ref, f32[32,128]{1,0:T(8,128)S(1)} %get-tuple-element.25.b1_ref), custom_call_target="tpu_custom_call" | custom-call | flops 1048576 | bytes 1048576 | tf_op jit(solution)/shard_map/pallas_call | solution.py:407
  104.6 15.7 %all-to-all-done.5.in_ref = f32[16,128,128]{2,1,0:T(8,128)S(1)} async-done(((f32[16,128,128]{2,1,0:T(8,128)}), f32[16,128,128]{2,1,0:T(8,128)S(1)}, u32[]{:S(2)}, u32[]{:S(2)}) %all-to-all-start.5) | async-done | bytes 1048608 | tf_op jit(solution)/shard_map/all_to_all | solution.py:418
  120.2 0.0 copy-done
  120.2 0.0 copy-done.3
  120.2 3.4 %shard_map.155 = (f32[4,16,16,512]{3,2,1,0:T(8,128)}, f32[64,64]{1,0:T(8,128)}) custom-call(f32[16,128,128]{2,1,0:T(8,128)S(1)} %all-to-all-done.5.in_ref, f32[4,16,16,512]{3,2,1,0:T(8,128)S(1)} %bitcast.18, bf16[256,256]{1,0:T(8,128)(2,1)S(1)} %copy-done.3), custom_call_target="tpu_custom_call" | custom-call | tf_op jit(solution)/shard_map/pallas_call | solution.py:492
  (5 shorter events, 0.0 us)
Async XLA Ops:
  6.0 35.5 %all-to-all-start = ((f32[16,240,128]{2,1,0:T(8,128)}), f32[16,240,128]{2,1,0:T(8,128)S(1)}, u32[]{:S(2)}, u32[]{:S(2)}) async-start(f32[16,240,128]{2,1,0:T(8,128)} %shard_map.148), calls=%async_computation | async-start | bytes 3932160 | tf_op jit(solution)/shard_map/all_to_all | solution.py:418
  14.5 27.1 %copy-start.4 = (bf16[128,512]{1,0:T(8,128)(2,1)S(1)}, bf16[128,512]{1,0:T(8,128)(2,1)}, u32[]{:S(2)}) copy-start(bf16[128,512]{1,0:T(8,128)(2,1)} %constant.17.clone.table_ref) | copy-start | bytes 393220
  14.5 27.1 %copy-start.6 = (bf16[128,256]{1,0:T(8,128)(2,1)S(1)}, bf16[128,256]{1,0:T(8,128)(2,1)}, u32[]{:S(2)}) copy-start(bf16[128,256]{1,0:T(8,128)(2,1)} %constant.18.clone.real_ref) | copy-start | bytes 196612
  21.6 37.0 %copy-start.7 = (bf16[64,256]{1,0:T(8,128)(2,1)S(1)}, bf16[64,256]{1,0:T(8,128)(2,1)}, u32[]{:S(2)}) copy-start(bf16[64,256]{1,0:T(8,128)(2,1)} %constant.20.clone.table_ref) | copy-start | bytes 98308
  21.6 37.0 %copy-start.8 = (f32[64,128]{1,0:T(8,128)S(1)}, f32[64,128]{1,0:T(8,128)}, u32[]{:S(2)}) copy-start(f32[64,128]{1,0:T(8,128)} %get-tuple-element.18.mix_ref) | copy-start | bytes 98308
  21.6 37.0 %copy-start.9 = (f32[32,128]{1,0:T(8,128)S(1)}, f32[32,128]{1,0:T(8,128)}, u32[]{:S(2)}) copy-start(f32[32,128]{1,0:T(8,128)} %constant.19.clone.tw_ref) | copy-start | bytes 49156
  21.6 51.4 %copy-start.1 = (f32[2,2,8,64,128]{4,3,2,1,0:T(8,128)S(1)}, f32[2,2,8,64,128]{4,3,2,1,0:T(8,128)}, u32[]{:S(2)}) copy-start(f32[2,2,8,64,128]{4,3,2,1,0:T(8,128)} %param.17) | copy-start | bytes 3145732
  41.5 42.7 %copy-start.5 = (bf16[192,256]{1,0:T(8,128)(2,1)S(1)}, bf16[192,256]{1,0:T(8,128)(2,1)}, u32[]{:S(2)}) copy-start(bf16[192,256]{1,0:T(8,128)(2,1)} %constant.21.clone.t_ref) | copy-start | bytes 294916
  42.2 53.8 %copy-start.2 = (bf16[512,192]{1,0:T(8,128)(2,1)S(1)}, bf16[512,192]{1,0:T(8,128)(2,1)}, u32[]{:S(2)}) copy-start(bf16[512,192]{1,0:T(8,128)(2,1)} %constant.22.clone.t_ref) | copy-start | bytes 589828
  96.1 24.2 %copy-start = (f32[1024,512]{1,0:T(8,128)S(1)}, f32[1024,512]{1,0:T(8,128)}, u32[]{:S(2)}) copy-start(f32[1024,512]{1,0:T(8,128)} %get-tuple-element.21) | copy-start | bytes 6291460
  96.1 24.2 %copy-start.3 = (bf16[256,256]{1,0:T(8,128)(2,1)S(1)}, bf16[256,256]{1,0:T(8,128)(2,1)}, u32[]{:S(2)}) copy-start(bf16[256,256]{1,0:T(8,128)(2,1)} %constant.23.clone.table_hbm) | copy-start | bytes 393220
  97.5 22.7 %all-to-all-start.5 = ((f32[16,128,128]{2,1,0:T(8,128)}), f32[16,128,128]{2,1,0:T(8,128)S(1)}, u32[]{:S(2)}, u32[]{:S(2)}) async-start(f32[16,128,128]{2,1,0:T(8,128)} %shard_map.154), calls=%async_computation.5 | async-start | bytes 2097152 | tf_op jit(solution)/shard_map/all_to_all | solution.py:418

commit v4 on v3

--- a/solution.py
+++ b/solution.py
@@ -18,8 +18,8 @@
 N = 16
 ROWS = 240
 HALF = ROWS // 2
-PER = 4
-PARTS = N // PER
+START_PARTS = (4, 4, 4, 4)
+END_PARTS = (4, 4, 4, 4)
 F32 = jnp.float32
 BF16 = jnp.bfloat16
 
@@ -96,6 +96,10 @@
     t = angle(frequency(p)[:, None], np.arange(256)[None, :], 256)
     full = np.stack([np.cos(t), np.sin(t)], 0).reshape(2, 16, 2, 256)
     return full.transpose(0, 2, 1, 3).reshape(64, 256)
+
+
+def spans(sizes):
+    return [(sum(sizes[:i]), size) for i, size in enumerate(sizes)]
 
 
 def split(values):
@@ -162,8 +166,8 @@
 
 def start_kernel(x_hbm, pre_hbm, cot_hbm, table_ref, out_hbm, x, pre, cot, out, in_sems, out_sems):
     moves = []
-    for i in range(PARTS):
-        at = pl.ds(PER * i, PER)
+    for i, (first, size) in enumerate(spans(START_PARTS)):
+        at = pl.ds(first, size)
         three = [
             pltpu.make_async_copy(a.at[:, at], b.at[:, at], in_sems.at[n, i])
             for n, (a, b) in enumerate([(pre_hbm, pre), (cot_hbm, cot), (x_hbm, x)])
@@ -173,15 +177,15 @@
         moves.append(three)
     both = table_ref[...]
     sends = []
-    for i in range(PARTS):
+    for i, (first, size) in enumerate(spans(START_PARTS)):
         for move in moves[i]:
             move.wait()
-        own = slice(PER * i, PER * i + PER)
+        own = slice(first, first + size)
         grad = cot[:, own] * slope(pre[:, own])
-        for j in range(0, PER, 2):
+        for j in range(0, size, 2):
             rows = []
             for n in (j, j + 1):
-                rows += [x[c, PER * i + n] for c in range(4)] + [grad[c, n] for c in range(4)]
+                rows += [x[c, first + n] for c in range(4)] + [grad[c, n] for c in range(4)]
             rows = jnp.concatenate(rows, axis=0)
             for half in range(2):
                 high, low = split(rows[:, 256 * half : 256 * half + 256])
@@ -189,8 +193,8 @@
                 done = two[:HALF] + (two[HALF:] + dot(both[:HALF], low, ((1,), (1,))))
                 for n in range(2):
                     at = slice(HALF * half, HALF * half + HALF)
-                    out[PER * i + j + n, at] = done[:, 128 * n : 128 * n + 128]
-        at = pl.ds(PER * i, PER)
+                    out[first + j + n, at] = done[:, 128 * n : 128 * n + 128]
+        at = pl.ds(first, size)
         send = pltpu.make_async_copy(out.at[at], out_hbm.at[at], out_sems.at[i])
         send.start()
         sends.append(send)
@@ -322,44 +326,31 @@
         out_ref[y, 8:12, 0:64] = mix[:, :64]
 
 
-def end_kernel(
-    in_ref, direct_hbm, table_hbm, out_hbm, mix_hbm, direct, table, out, mix, sems, in_sems, out_sems
-):
-    table_move = pltpu.make_async_copy(table_hbm, table, sems.at[0])
-    table_move.start()
-    moves = []
-    for i in range(PARTS):
-        at = pl.ds(PER * i, PER)
-        move = pltpu.make_async_copy(direct_hbm.at[:, at], direct.at[:, at], in_sems.at[i])
-        move.start()
-        moves.append(move)
+def end_kernel(in_ref, direct_ref, table_ref, out_hbm, mix_hbm, out, mix, mix_sem, out_sems):
     for d in range(16):
         mix[4 * d : 4 * d + 4] = in_ref[d, 8:12, 0:64] * (1.0 / math.sqrt(CELLS))
-    mix_move = pltpu.make_async_copy(mix, mix_hbm, sems.at[1])
+    mix_move = pltpu.make_async_copy(mix, mix_hbm, mix_sem)
     mix_move.start()
     sends = []
-    for i in range(PARTS):
+    for i, (first, size) in enumerate(spans(END_PARTS)):
         rows = [[], []]
-        for j in range(PER):
-            turned = in_ref[PER * i + j].T
+        for j in range(size):
+            turned = in_ref[first + j].T
             for half in range(2):
                 at = slice(64 * half, 64 * half + 64)
                 rows[half].append(jnp.concatenate([turned[:64, at], turned[64:, at]], axis=1))
-        if i == 0:
-            table_move.wait()
         parts = []
         for half in range(2):
             high, low = split(jnp.concatenate(rows[half], axis=0))
             parts.append(
-                dot(jnp.concatenate([high, high], axis=1), table[...]) + dot(low, table[:128])
+                dot(jnp.concatenate([high, high], axis=1), table_ref[...]) + dot(low, table_ref[:128])
             )
         done = jnp.concatenate(parts, axis=1)
-        moves[i].wait()
-        for j in range(PER):
+        for j in range(size):
             for c in range(4):
                 at = 64 * j + 16 * c
-                out[c, PER * i + j] = direct[c, PER * i + j] + done[at : at + 16]
-        at = pl.ds(PER * i, PER)
+                out[c, first + j] = direct_ref[c, first + j] + done[at : at + 16]
+        at = pl.ds(first, size)
         send = pltpu.make_async_copy(out.at[:, at], out_hbm.at[:, at], out_sems.at[i])
         send.start()
         sends.append(send)
@@ -437,8 +428,8 @@
             field,
             field,
             pltpu.VMEM((N, ROWS, 128), F32),
-            pltpu.SemaphoreType.DMA((3, PARTS)),
-            pltpu.SemaphoreType.DMA((PARTS,)),
+            pltpu.SemaphoreType.DMA((3, len(START_PARTS))),
+            pltpu.SemaphoreType.DMA((len(START_PARTS),)),
         ],
         compiler_params=params(60),
     )(*shaped, column(depth_sent()))
@@ -483,6 +474,7 @@
         first_back_kernel, struct(288, 128), (mode_back, jnp.asarray(first_table), mix)
     )
     first_back = exchange(first_back.reshape(16, 1, 2304), "px").reshape(288, 128)
+    first_back, spectral_grad = lax.optimization_barrier((first_back, spectral_grad))
     second_back = call(
         second_back_kernel,
         struct(16, 128, 128),
@@ -492,16 +484,13 @@
     input_grad, mix_grad = pl.pallas_call(
         end_kernel,
         out_shape=(struct(4, N, N, 512), struct(C, C)),
-        in_specs=whole(1) + [anywhere] * 2,
+        in_specs=whole(3),
         out_specs=(anywhere, anywhere),
         scratch_shapes=[
             field,
-            pltpu.VMEM((256, 256), BF16),
-            field,
             pltpu.VMEM((C, C), F32),
-            pltpu.SemaphoreType.DMA((2,)),
-            pltpu.SemaphoreType.DMA((PARTS,)),
-            pltpu.SemaphoreType.DMA((PARTS,)),
+            pltpu.SemaphoreType.DMA,
+            pltpu.SemaphoreType.DMA((len(END_PARTS),)),
         ],
         compiler_params=params(20),
     )(gathered, direct.reshape(4, N, N, 512), column(depth_inverse()))

time: 124 us -> 121 us (0.976)
  blocking collectives: 52.1 us -> 62.3 us
  waiting for transfers between devices: 35.6 us -> 25.7 us
  Pallas kernels: 21.3 us -> 19.7 us
  starting transfers between devices: 13.9 us -> 12.5 us
    all_to_all x4, blocking collectives: 52.1 us -> 62.3 us  [exchange(): return lax.all_to_all(values, axis, split_axis=0, concat_axis=0, tiled=True)]
    all_to_all x2, waiting for transfers between devices: 35.6 us -> 25.7 us  [exchange(): return lax.all_to_all(values, axis, split_axis=0, concat_axis=0, tiled=True)]
    all_to_all x2, starting transfers between devices: 13.9 us -> 12.5 us  [exchange(): return lax.all_to_all(values, axis, split_axis=0, concat_axis=0, tiled=True)]
    pallas_call x1, Pallas kernels: 3.4 us -> 2.1 us  [per_device(): pl.pallas_call(end_kernel, out_shape=(struct(4, N, N, 512), struct(C, C))...]
where the time goes in v4:
time: 121 us
  blocking collectives  62.3 us (51%)
  waiting for transfers between devices  25.7 us (21%)
  Pallas kernels  19.7 us (16%)
  starting transfers between devices  12.5 us (10%)
    all_to_all x4, blocking collectives, exchange(): return lax.all_to_all(values, axis, split_axis=0, concat_axis=0, tiled=True)  62.3 us
    all_to_all x2, waiting for transfers between devices, exchange(): return lax.all_to_all(values, axis, split_axis=0, concat_axis=0, tiled=True)  25.7 us
    all_to_all x2, starting transfers between devices, exchange(): return lax.all_to_all(values, axis, split_axis=0, concat_axis=0, tiled=True)  12.5 us
    pallas_call x1, Pallas kernels, per_device(): pl.pallas_call(side_kernel, grid=(4,), out_shape=(struct(1024, 512), stru...  7.09 us
    pallas_call x1, Pallas kernels, per_device(): pl.pallas_call(start_kernel, out_shape=struct(N, ROWS, 128), in_specs=[an...  5.36 us
    pallas_call x6, Pallas kernels, call(): pl.pallas_call(body, out_shape=outs, in_specs=whole(len(args)), out_specs...  5.11 us
  transfers between devices with their start and end apart: 2, of which 2 were waited for; matrix products, arithmetic and copies ran while one was open for 0% of the time, Pallas kernels for 7%

profile of v4, /device:TPU:1, one launch (start us, length us, event | category | flops | bytes accessed | tf_op | source)
XLA Modules:
  0.0 120.9 jit_solution(4769936116586287571)
XLA Ops:
  0.6 5.4 %shard_map.148 = f32[16,240,128]{2,1,0:T(8,128)} custom-call(f32[4,16,16,512]{3,2,1,0:T(8,128)} %bitcast.27, f32[4,16,16,512]{3,2,1,0:T(8,128)} %bitcast.29, f32[4,16,16,512]{3,2,1,0:T(8,128)} %bitcast.31, bf16[240,256]{1,0:T(8,128)(2,1)} %constant.16.clone.table_ref), custom_call_target="tpu_custom_call" | custom-call | tf_op jit(solution)/shard_map/pallas_call | solution.py:421
  6.0 8.5 %all-to-all-start = ((f32[16,240,128]{2,1,0:T(8,128)}), f32[16,240,128]{2,1,0:T(8,128)S(1)}, u32[]{:S(2)}, u32[]{:S(2)}) async-start(f32[16,240,128]{2,1,0:T(8,128)} %shard_map.148), calls=%async_computation | async-start | bytes 3932160 | tf_op jit(solution)/shard_map/all_to_all | solution.py:409
  14.5 0.0 copy-start.6
  14.5 7.1 %shard_map.149 = (f32[1024,512]{1,0:T(8,128)}, f32[64,128]{1,0:T(8,128)}) custom-call(f32[1024,512]{1,0:T(8,128)} %bitcast.28, f32[1024,512]{1,0:T(8,128)} %bitcast.30, f32[1024,512]{1,0:T(8,128)} %bitcast.32, f32[64,64]{1,0:T(8,128)} %weight_ref.1), custom_call_target="tpu_custom_call" | custom-call | flops 1073741824 | bytes 6291456 | tf_op jit(solution)/shard_map/pallas_call | solution.py:438
  21.6 0.0 copy-start.9
  21.6 0.0 copy-start.1
  21.6 19.9 %all-to-all-done.in_ref = f32[16,240,128]{2,1,0:T(8,128)S(1)} async-done(((f32[16,240,128]{2,1,0:T(8,128)}), f32[16,240,128]{2,1,0:T(8,128)S(1)}, u32[]{:S(2)}, u32[]{:S(2)}) %all-to-all-start) | async-done | bytes 1966112 | tf_op jit(solution)/shard_map/all_to_all | solution.py:409
  41.5 0.0 copy-done.4
  41.5 0.0 copy-done.6
  41.5 0.7 shard_map.150
  42.2 0.0 copy-start.2
  42.2 16.3 %all_to_all.30 = f32[16,32,128]{2,1,0:T(8,128)S(1)} all-to-all(f32[16,32,128]{2,1,0:T(8,128)S(1)} %bitcast.19), channel_id=1, replica_groups=mesh['px'=16,'py'=16] {'px'}, dimensions={0} | all-to-all | bytes 524288 | tf_op jit(solution)/shard_map/all_to_all | solution.py:409
  58.6 0.0 copy-done.7
  58.6 0.0 copy-done.8
  58.6 0.0 copy-done.9
  58.6 0.4 shard_map.151
  59.0 14.1 %all_to_all.31 = f32[16,16,128]{2,1,0:T(8,128)S(1)} all-to-all(f32[16,16,128]{2,1,0:T(8,128)S(1)} %bitcast.24), channel_id=1, replica_groups=mesh['px'=16,'py'=16] {'py'}, dimensions={0} | all-to-all | bytes 262144 | tf_op jit(solution)/shard_map/all_to_all | solution.py:409
  73.0 0.0 copy-done.1
  73.0 0.7 shard_map.152
  73.8 10.4 %all_to_all.32 = f32[16,4,128]{2,1,0:T(4,128)S(1)} all-to-all(f32[16,4,128]{2,1,0:T(4,128)S(1)} %bitcast.26), channel_id=1, replica_groups=mesh['px'=16,'py'=16] {'py'}, dimensions={0} | all-to-all | bytes 65536 | tf_op jit(solution)/shard_map/all_to_all | solution.py:409
  84.2 0.0 copy-done.5
  84.2 1.2 %shard_map.153 = f32[288,128]{1,0:T(8,128)} custom-call(f32[64,128]{1,0:T(8,128)S(1)} %bitcast.25, bf16[192,256]{1,0:T(8,128)(2,1)S(1)} %copy-done.5, f32[2,128]{1,0:T(2,128)S(1)} %get-tuple-element.22.mix_ref), custom_call_target="tpu_custom_call" | custom-call | tf_op jit(solution)/shard_map/pallas_call | solution.py:398
  85.4 4.0 %all-to-all-start.4 = ((f32[16,1,2304]{2,1,0:T(1,128)}), f32[16,1,2304]{2,1,0:T(1,128)S(1)}, u32[]{:S(2)}, u32[]{:S(2)}) async-start(f32[16,1,2304]{2,1,0:T(1,128)} %bitcast.13), calls=%async_computation.4 | async-start | bytes 294912 | tf_op jit(solution)/shard_map/all_to_all | solution.py:409
  89.5 0.0 copy-start
  89.5 0.0 copy-start.3
  89.5 1.6 %shard_map.154 = f32[2048,128]{1,0:T(8,128)} custom-call(f32[64,128]{1,0:T(8,128)S(1)} %get-tuple-element.23.xr_ref, f32[64,128]{1,0:T(8,128)S(1)} %get-tuple-element.24.xi_ref, f32[32,128]{1,0:T(8,128)S(1)} %get-tuple-element.25.b1_ref), custom_call_target="tpu_custom_call" | custom-call | flops 1048576 | bytes 1048576 | tf_op jit(solution)/shard_map/pallas_call | solution.py:398
  91.1 5.8 %all-to-all-done.4 = f32[16,1,2304]{2,1,0:T(1,128)S(1)} async-done(((f32[16,1,2304]{2,1,0:T(1,128)}), f32[16,1,2304]{2,1,0:T(1,128)S(1)}, u32[]{:S(2)}, u32[]{:S(2)}) %all-to-all-start.4) | async-done | bytes 147488 | tf_op jit(solution)/shard_map/all_to_all | solution.py:409
  96.9 0.0 copy-done.2
  96.9 0.4 shard_map.155
  97.4 21.5 %all_to_all.33.in_ref = f32[16,128,128]{2,1,0:T(8,128)S(1)} all-to-all(f32[16,128,128]{2,1,0:T(8,128)S(1)} %shard_map.155), channel_id=1, replica_groups=mesh['px'=16,'py'=16] {'py'}, dimensions={0} | all-to-all | bytes 2097152 | tf_op jit(solution)/shard_map/all_to_all | solution.py:409
  118.8 0.0 copy-done
  118.8 2.1 %shard_map.156 = (f32[4,16,16,512]{3,2,1,0:T(8,128)}, f32[64,64]{1,0:T(8,128)}) custom-call(f32[16,128,128]{2,1,0:T(8,128)S(1)} %all_to_all.33.in_ref, f32[4,16,16,512]{3,2,1,0:T(8,128)S(1)} %bitcast.18, bf16[256,256]{1,0:T(8,128)(2,1)S(1)} %copy-done.3), custom_call_target="tpu_custom_call" | custom-call | tf_op jit(solution)/shard_map/pallas_call | solution.py:484
  (5 shorter events, 0.0 us)
Async XLA Ops:
  6.0 35.5 %all-to-all-start = ((f32[16,240,128]{2,1,0:T(8,128)}), f32[16,240,128]{2,1,0:T(8,128)S(1)}, u32[]{:S(2)}, u32[]{:S(2)}) async-start(f32[16,240,128]{2,1,0:T(8,128)} %shard_map.148), calls=%async_computation | async-start | bytes 3932160 | tf_op jit(solution)/shard_map/all_to_all | solution.py:409
  14.5 27.1 %copy-start.4 = (bf16[128,512]{1,0:T(8,128)(2,1)S(1)}, bf16[128,512]{1,0:T(8,128)(2,1)}, u32[]{:S(2)}) copy-start(bf16[128,512]{1,0:T(8,128)(2,1)} %constant.17.clone.table_ref) | copy-start | bytes 393220
  14.5 27.1 %copy-start.6 = (bf16[128,256]{1,0:T(8,128)(2,1)S(1)}, bf16[128,256]{1,0:T(8,128)(2,1)}, u32[]{:S(2)}) copy-start(bf16[128,256]{1,0:T(8,128)(2,1)} %constant.18.clone.real_ref) | copy-start | bytes 196612
  21.6 37.0 %copy-start.7 = (bf16[64,256]{1,0:T(8,128)(2,1)S(1)}, bf16[64,256]{1,0:T(8,128)(2,1)}, u32[]{:S(2)}) copy-start(bf16[64,256]{1,0:T(8,128)(2,1)} %constant.20.clone.table_ref) | copy-start | bytes 98308
  21.6 37.0 %copy-start.8 = (f32[64,128]{1,0:T(8,128)S(1)}, f32[64,128]{1,0:T(8,128)}, u32[]{:S(2)}) copy-start(f32[64,128]{1,0:T(8,128)} %get-tuple-element.20.mix_ref) | copy-start | bytes 98308
  21.6 37.0 %copy-start.9 = (f32[32,128]{1,0:T(8,128)S(1)}, f32[32,128]{1,0:T(8,128)}, u32[]{:S(2)}) copy-start(f32[32,128]{1,0:T(8,128)} %constant.19.clone.tw_ref) | copy-start | bytes 49156
  21.6 51.4 %copy-start.1 = (f32[2,2,8,64,128]{4,3,2,1,0:T(8,128)S(1)}, f32[2,2,8,64,128]{4,3,2,1,0:T(8,128)}, u32[]{:S(2)}) copy-start(f32[2,2,8,64,128]{4,3,2,1,0:T(8,128)} %param.17) | copy-start | bytes 3145732
  41.5 42.7 %copy-start.5 = (bf16[192,256]{1,0:T(8,128)(2,1)S(1)}, bf16[192,256]{1,0:T(8,128)(2,1)}, u32[]{:S(2)}) copy-start(bf16[192,256]{1,0:T(8,128)(2,1)} %constant.21.clone.t_ref) | copy-start | bytes 294916
  42.2 54.7 %copy-start.2 = (bf16[512,192]{1,0:T(8,128)(2,1)S(1)}, bf16[512,192]{1,0:T(8,128)(2,1)}, u32[]{:S(2)}) copy-start(bf16[512,192]{1,0:T(8,128)(2,1)} %constant.22.clone.t_ref) | copy-start | bytes 589828
  85.4 11.5 %all-to-all-start.4 = ((f32[16,1,2304]{2,1,0:T(1,128)}), f32[16,1,2304]{2,1,0:T(1,128)S(1)}, u32[]{:S(2)}, u32[]{:S(2)}) async-start(f32[16,1,2304]{2,1,0:T(1,128)} %bitcast.13), calls=%async_computation.4 | async-start | bytes 294912 | tf_op jit(solution)/shard_map/all_to_all | solution.py:409
  89.5 29.4 %copy-start = (f32[1024,512]{1,0:T(8,128)S(1)}, f32[1024,512]{1,0:T(8,128)}, u32[]{:S(2)}) copy-start(f32[1024,512]{1,0:T(8,128)} %get-tuple-element.27) | copy-start | bytes 6291460
  89.5 29.3 %copy-start.3 = (bf16[256,256]{1,0:T(8,128)(2,1)S(1)}, bf16[256,256]{1,0:T(8,128)(2,1)}, u32[]{:S(2)}) copy-start(bf16[256,256]{1,0:T(8,128)(2,1)} %constant.23.clone.table_ref) | copy-start | bytes 393220

commit v5 on v4

--- a/solution.py
+++ b/solution.py
@@ -225,14 +225,17 @@
         rows.append(jnp.concatenate([re * c + im * s, im * c - re * s], axis=1))
     data = split(jnp.concatenate(rows, axis=0))
     done = dot3((table_ref[:32], table_ref[32:]), data, ((1,), (1,)))
+    lane = lanes((2, 128))
     for h in range(2):
-        for b in range(8):
-            tile = done[16 * h : 16 * h + 16, 128 * (b // 4) : 128 * (b // 4) + 128]
-            if b % 4:
-                tile = pltpu.roll(tile, 128 - 32 * (b % 4), 1)
-            d = 8 * h + b
-            out_ref[16 * d : 16 * d + 16] = tile
-            out_ref[16 * d : 16 * d + 4, 64:128] = mix_ref[4 * d : 4 * d + 4, 64:128]
+        for t in range(2):
+            tile = slice(128 * t, 128 * t + 128)
+            blocks = [done[16 * h + 4 * g : 16 * h + 4 * g + 4, tile] for g in range(4)]
+            for b, block in enumerate(transpose_groups(blocks, 32)):
+                d = 8 * h + 4 * t + b
+                out_ref[6 * d : 6 * d + 4] = block
+                out_ref[6 * d + 4 : 6 * d + 6] = jnp.where(
+                    lane < 64, mix_ref[4 * d : 4 * d + 2], mix_ref[4 * d + 2 : 4 * d + 4]
+                )
 
 
 def swap_halves(b1):
@@ -240,13 +243,11 @@
     return jnp.where(lanes(b1.shape) < 64, turned, -turned)
 
 
-def mode_kernel(in_ref, w_ref, out_ref, xr_ref, xi_ref, b1_ref, mix_ref):
-    def field(ri, f):
-        return jnp.concatenate(
-            [in_ref[pl.ds(8 * ri + 4 * f + c, 16, stride=16), :] for c in range(4)], axis=0
-        )
-
-    spread = jnp.concatenate([field(0, 1), field(1, 1)], axis=0).T[:32]
+def mode_kernel(in_ref, w_ref, out_ref, fields_ref, b1_ref, mix_ref):
+    fields = jnp.concatenate([in_ref[pl.ds(c, 16, stride=6), :] for c in range(4)], axis=0)
+    fields_ref[...] = fields
+    turned = jnp.concatenate([fields, fields], axis=0).T
+    spread = jnp.where(lanes((32, 128)) < 64, turned[32:64], turned[96:])
     mode = lax.broadcasted_iota(jnp.int32, (32, 128), 0)
     b1 = spread * jnp.where((mode // 2) % 8 == 0, 1.0 / CELLS, 2.0 / CELLS)
     b2 = swap_halves(b1)
@@ -263,22 +264,21 @@
         total = jnp.where(lane == place + 2, imag, total)
     for c in range(4):
         out_ref[pl.ds(c, 16, stride=4), :] = total[16 * c : 16 * c + 16]
-    xr_ref[...] = field(0, 0)
-    xi_ref[...] = field(1, 0)
     b1_ref[...] = b1
-    mix = in_ref[0:4]
+    mix = in_ref[4:6]
     for s in range(1, 16):
-        mix = mix + in_ref[16 * s : 16 * s + 4]
-    mix_ref[...] = jnp.where(lanes((2, 128)) < 64, pltpu.roll(mix, 64, 1)[:2], mix[2:])
-
-
-def outer_kernel(xr_ref, xi_ref, b1_ref, out_ref):
-    xr, xi, b1 = xr_ref[...], xi_ref[...], b1_ref[...]
+        mix = mix + in_ref[6 * s + 4 : 6 * s + 6]
+    mix_ref[...] = mix
+
+
+def outer_kernel(fields_ref, b1_ref, out_ref):
+    fields, b1 = fields_ref[...], b1_ref[...]
     b2 = swap_halves(b1)
     for m in range(32):
         p, k, q = m // 16, (m // 2) % 8, m % 2
         at = ((p * 2 + q) * 8 + k) * 64
-        out_ref[at : at + 64] = xr[:, m : m + 1] * b1[m : m + 1] + xi[:, m : m + 1] * b2[m : m + 1]
+        real, imag = fields[:, m : m + 1], fields[:, 64 + m : 65 + m]
+        out_ref[at : at + 64] = real * b1[m : m + 1] + imag * b2[m : m + 1]
 
 
 def first_back_kernel(in_ref, t_ref, mix_ref, out_ref):
@@ -451,20 +451,20 @@
     along_second = exchange(along_second.reshape(16, 32, 128), "px").reshape(512, 128)
     along_first = call(
         first_kernel,
-        struct(256, 128),
+        struct(96, 128),
         (along_second, jnp.asarray(first_twiddle()), column(first_halves()), mix),
     )
-    spectra = exchange(along_first.reshape(16, 16, 128), "py").reshape(256, 128)
-    mode_back, xr, xi, b1, mix = call(
+    spectra = exchange(along_first.reshape(16, 1, 768), "py").reshape(96, 128)
+    mode_back, fields, b1, mix = call(
         mode_kernel,
-        (struct(64, 128), struct(64, 128), struct(64, 128), struct(32, 128), struct(2, 128)),
+        (struct(64, 128), struct(64, 128), struct(32, 128), struct(2, 128)),
         (spectra, spectral_weight.reshape(2048, 128)),
     )
     mode_back = exchange(mode_back.reshape(16, 4, 128), "py").reshape(64, 128)
     spectral_grad = call(
         outer_kernel,
         struct(2048, 128),
-        (xr, xi, b1),
+        (fields, b1),
         8,
         pl.CostEstimate(flops=1 << 20, bytes_accessed=1 << 20, transcendentals=0),
     ).reshape(spectral_weight.shape)

time: 121 us -> 121 us (level)
  no operation moved by 1% of the time
where the time goes in v5:
time: 121 us; the launch traced here: 120 us
  blocking collectives  61.7 us (51%)
  waiting for transfers between devices  25.7 us (21%)
  Pallas kernels  19.8 us (16%)
  starting transfers between devices  12.5 us (10%)
    all_to_all x4, blocking collectives, exchange(): return lax.all_to_all(values, axis, split_axis=0, concat_axis=0, tiled=True)  61.7 us
    all_to_all x2, waiting for transfers between devices, exchange(): return lax.all_to_all(values, axis, split_axis=0, concat_axis=0, tiled=True)  25.7 us
    all_to_all x2, starting transfers between devices, exchange(): return lax.all_to_all(values, axis, split_axis=0, concat_axis=0, tiled=True)  12.5 us
    pallas_call x1, Pallas kernels, per_device(): pl.pallas_call(side_kernel, grid=(4,), out_shape=(struct(1024, 512), stru...  7.09 us
    pallas_call x1, Pallas kernels, per_device(): pl.pallas_call(start_kernel, out_shape=struct(N, ROWS, 128), in_specs=[an...  5.36 us
    pallas_call x6, Pallas kernels, call(): pl.pallas_call(body, out_shape=outs, in_specs=whole(len(args)), out_specs...  5.26 us
  transfers between devices with their start and end apart: 2, of which 2 were waited for; matrix products, arithmetic and copies ran while one was open for 0% of the time, Pallas kernels for 7%

profile of v5, /device:TPU:1, one launch (start us, length us, event | category | flops | bytes accessed | tf_op | source)
XLA Modules:
  0.0 120.5 jit_solution(8049429278283150415)
XLA Ops:
  0.6 5.4 %shard_map.148 = f32[16,240,128]{2,1,0:T(8,128)} custom-call(f32[4,16,16,512]{3,2,1,0:T(8,128)} %bitcast.27, f32[4,16,16,512]{3,2,1,0:T(8,128)} %bitcast.29, f32[4,16,16,512]{3,2,1,0:T(8,128)} %bitcast.31, bf16[240,256]{1,0:T(8,128)(2,1)} %constant.16.clone.table_ref), custom_call_target="tpu_custom_call" | custom-call | tf_op jit(solution)/shard_map/pallas_call | solution.py:421
  6.0 8.5 %all-to-all-start = ((f32[16,240,128]{2,1,0:T(8,128)}), f32[16,240,128]{2,1,0:T(8,128)S(1)}, u32[]{:S(2)}, u32[]{:S(2)}) async-start(f32[16,240,128]{2,1,0:T(8,128)} %shard_map.148), calls=%async_computation | async-start | bytes 3932160 | tf_op jit(solution)/shard_map/all_to_all | solution.py:409
  14.5 0.0 copy-start.6
  14.5 7.1 %shard_map.149 = (f32[1024,512]{1,0:T(8,128)}, f32[64,128]{1,0:T(8,128)}) custom-call(f32[1024,512]{1,0:T(8,128)} %bitcast.28, f32[1024,512]{1,0:T(8,128)} %bitcast.30, f32[1024,512]{1,0:T(8,128)} %bitcast.32, f32[64,64]{1,0:T(8,128)} %weight_ref.1), custom_call_target="tpu_custom_call" | custom-call | flops 1073741824 | bytes 6291456 | tf_op jit(solution)/shard_map/pallas_call | solution.py:438
  21.6 0.0 copy-start.9
  21.6 0.0 copy-start.1
  21.6 19.9 %all-to-all-done.in_ref = f32[16,240,128]{2,1,0:T(8,128)S(1)} async-done(((f32[16,240,128]{2,1,0:T(8,128)}), f32[16,240,128]{2,1,0:T(8,128)S(1)}, u32[]{:S(2)}, u32[]{:S(2)}) %all-to-all-start) | async-done | bytes 1966112 | tf_op jit(solution)/shard_map/all_to_all | solution.py:409
  41.5 0.0 copy-done.4
  41.5 0.0 copy-done.6
  41.5 0.7 shard_map.150
  42.2 0.0 copy-start.2
  42.2 16.3 %all_to_all.30 = f32[16,32,128]{2,1,0:T(8,128)S(1)} all-to-all(f32[16,32,128]{2,1,0:T(8,128)S(1)} %bitcast.19), channel_id=1, replica_groups=mesh['px'=16,'py'=16] {'px'}, dimensions={0} | all-to-all | bytes 524288 | tf_op jit(solution)/shard_map/all_to_all | solution.py:409
  58.6 0.0 copy-done.7
  58.6 0.0 copy-done.8
  58.6 0.0 copy-done.9
  58.6 0.5 shard_map.151
  59.0 13.7 %all_to_all.31 = f32[16,1,768]{2,1,0:T(1,128)S(1)} all-to-all(f32[16,1,768]{2,1,0:T(1,128)S(1)} %bitcast.24), channel_id=1, replica_groups=mesh['px'=16,'py'=16] {'py'}, dimensions={0} | all-to-all | bytes 98304 | tf_op jit(solution)/shard_map/all_to_all | solution.py:409
  72.8 0.0 copy-done.1
  72.8 0.8 shard_map.152
  73.5 10.1 %all_to_all.32 = f32[16,4,128]{2,1,0:T(4,128)S(1)} all-to-all(f32[16,4,128]{2,1,0:T(4,128)S(1)} %bitcast.26), channel_id=1, replica_groups=mesh['px'=16,'py'=16] {'py'}, dimensions={0} | all-to-all | bytes 65536 | tf_op jit(solution)/shard_map/all_to_all | solution.py:409
  83.7 0.0 copy-done.5
  83.7 1.2 %shard_map.153 = f32[288,128]{1,0:T(8,128)} custom-call(f32[64,128]{1,0:T(8,128)S(1)} %bitcast.25, bf16[192,256]{1,0:T(8,128)(2,1)S(1)} %copy-done.5, f32[2,128]{1,0:T(2,128)S(1)} %get-tuple-element.21.mix_ref), custom_call_target="tpu_custom_call" | custom-call | tf_op jit(solution)/shard_map/pallas_call | solution.py:398
  84.9 4.0 %all-to-all-start.4 = ((f32[16,1,2304]{2,1,0:T(1,128)}), f32[16,1,2304]{2,1,0:T(1,128)S(1)}, u32[]{:S(2)}, u32[]{:S(2)}) async-start(f32[16,1,2304]{2,1,0:T(1,128)} %bitcast.13), calls=%async_computation.4 | async-start | bytes 294912 | tf_op jit(solution)/shard_map/all_to_all | solution.py:409
  89.0 0.0 copy-start
  89.0 0.0 copy-start.3
  89.0 1.7 %shard_map.154 = f32[2048,128]{1,0:T(8,128)} custom-call(f32[64,128]{1,0:T(8,128)S(1)} %get-tuple-element.22.fields_ref, f32[32,128]{1,0:T(8,128)S(1)} %get-tuple-element.23.b1_ref), custom_call_target="tpu_custom_call" | custom-call | flops 1048576 | bytes 1048576 | tf_op jit(solution)/shard_map/pallas_call | solution.py:398
  90.7 5.7 %all-to-all-done.4 = f32[16,1,2304]{2,1,0:T(1,128)S(1)} async-done(((f32[16,1,2304]{2,1,0:T(1,128)}), f32[16,1,2304]{2,1,0:T(1,128)S(1)}, u32[]{:S(2)}, u32[]{:S(2)}) %all-to-all-start.4) | async-done | bytes 147488 | tf_op jit(solution)/shard_map/all_to_all | solution.py:409
  96.4 0.0 copy-done.2
  96.4 0.4 shard_map.155
  96.9 21.5 %all_to_all.33.in_ref = f32[16,128,128]{2,1,0:T(8,128)S(1)} all-to-all(f32[16,128,128]{2,1,0:T(8,128)S(1)} %shard_map.155), channel_id=1, replica_groups=mesh['px'=16,'py'=16] {'py'}, dimensions={0} | all-to-all | bytes 2097152 | tf_op jit(solution)/shard_map/all_to_all | solution.py:409
  118.3 0.0 copy-done
  118.3 2.1 %shard_map.156 = (f32[4,16,16,512]{3,2,1,0:T(8,128)}, f32[64,64]{1,0:T(8,128)}) custom-call(f32[16,128,128]{2,1,0:T(8,128)S(1)} %all_to_all.33.in_ref, f32[4,16,16,512]{3,2,1,0:T(8,128)S(1)} %bitcast.18, bf16[256,256]{1,0:T(8,128)(2,1)S(1)} %copy-done.3), custom_call_target="tpu_custom_call" | custom-call | tf_op jit(solution)/shard_map/pallas_call | solution.py:484
  (5 shorter events, 0.0 us)
Async XLA Ops:
  6.0 35.5 %all-to-all-start = ((f32[16,240,128]{2,1,0:T(8,128)}), f32[16,240,128]{2,1,0:T(8,128)S(1)}, u32[]{:S(2)}, u32[]{:S(2)}) async-start(f32[16,240,128]{2,1,0:T(8,128)} %shard_map.148), calls=%async_computation | async-start | bytes 3932160 | tf_op jit(solution)/shard_map/all_to_all | solution.py:409
  14.5 27.1 %copy-start.4 = (bf16[128,512]{1,0:T(8,128)(2,1)S(1)}, bf16[128,512]{1,0:T(8,128)(2,1)}, u32[]{:S(2)}) copy-start(bf16[128,512]{1,0:T(8,128)(2,1)} %constant.17.clone.table_ref) | copy-start | bytes 393220
  14.5 27.1 %copy-start.6 = (bf16[128,256]{1,0:T(8,128)(2,1)S(1)}, bf16[128,256]{1,0:T(8,128)(2,1)}, u32[]{:S(2)}) copy-start(bf16[128,256]{1,0:T(8,128)(2,1)} %constant.18.clone.real_ref) | copy-start | bytes 196612
  21.6 37.0 %copy-start.7 = (bf16[64,256]{1,0:T(8,128)(2,1)S(1)}, bf16[64,256]{1,0:T(8,128)(2,1)}, u32[]{:S(2)}) copy-start(bf16[64,256]{1,0:T(8,128)(2,1)} %constant.20.clone.table_ref) | copy-start | bytes 98308
  21.6 37.0 %copy-start.8 = (f32[64,128]{1,0:T(8,128)S(1)}, f32[64,128]{1,0:T(8,128)}, u32[]{:S(2)}) copy-start(f32[64,128]{1,0:T(8,128)} %get-tuple-element.19.mix_ref) | copy-start | bytes 98308
  21.6 37.0 %copy-start.9 = (f32[32,128]{1,0:T(8,128)S(1)}, f32[32,128]{1,0:T(8,128)}, u32[]{:S(2)}) copy-start(f32[32,128]{1,0:T(8,128)} %constant.19.clone.tw_ref) | copy-start | bytes 49156
  21.6 51.2 %copy-start.1 = (f32[2,2,8,64,128]{4,3,2,1,0:T(8,128)S(1)}, f32[2,2,8,64,128]{4,3,2,1,0:T(8,128)}, u32[]{:S(2)}) copy-start(f32[2,2,8,64,128]{4,3,2,1,0:T(8,128)} %param.17) | copy-start | bytes 3145732
  41.5 42.2 %copy-start.5 = (bf16[192,256]{1,0:T(8,128)(2,1)S(1)}, bf16[192,256]{1,0:T(8,128)(2,1)}, u32[]{:S(2)}) copy-start(bf16[192,256]{1,0:T(8,128)(2,1)} %constant.21.clone.t_ref) | copy-start | bytes 294916
  42.2 54.2 %copy-start.2 = (bf16[512,192]{1,0:T(8,128)(2,1)S(1)}, bf16[512,192]{1,0:T(8,128)(2,1)}, u32[]{:S(2)}) copy-start(bf16[512,192]{1,0:T(8,128)(2,1)} %constant.22.clone.t_ref) | copy-start | bytes 589828
  84.9 11.5 %all-to-all-start.4 = ((f32[16,1,2304]{2,1,0:T(1,128)}), f32[16,1,2304]{2,1,0:T(1,128)S(1)}, u32[]{:S(2)}, u32[]{:S(2)}) async-start(f32[16,1,2304]{2,1,0:T(1,128)} %bitcast.13), calls=%async_computation.4 | async-start | bytes 294912 | tf_op jit(solution)/shard_map/all_to_all | solution.py:409
  89.0 29.4 %copy-start = (f32[1024,512]{1,0:T(8,128)S(1)}, f32[1024,512]{1,0:T(8,128)}, u32[]{:S(2)}) copy-start(f32[1024,512]{1,0:T(8,128)} %get-tuple-element.25) | copy-start | bytes 6291460
  89.0 29.3 %copy-start.3 = (bf16[256,256]{1,0:T(8,128)(2,1)S(1)}, bf16[256,256]{1,0:T(8,128)(2,1)}, u32[]{:S(2)}) copy-start(bf16[256,256]{1,0:T(8,128)(2,1)} %constant.23.clone.table_ref) | copy-start | bytes 393220

commit v6 on v5

--- a/solution.py
+++ b/solution.py
@@ -203,18 +203,23 @@
 
 
 def second_kernel(in_ref, table_ref, real_ref, out_ref):
-    for k in range(8):
-        at, size = (0, 8) if k == 0 else (16 * k - 8, 16)
-        both = real_ref[...] if k == 0 else table_ref[...]
-        pieces = [(s, at + HALF * half) for s in range(16) for half in range(2)]
-        rows = jnp.concatenate([in_ref[s, a : a + size, :] for s, a in pieces], axis=0)
-        high, low = split(rows)
+    for group in ((0,), (1, 2), (3, 4), (5, 6), (7,)):
+        both = table_ref[...] if group[0] else real_ref[...]
+        columns = []
+        for k in group:
+            at, size = (0, 8) if k == 0 else (16 * k - 8, 16)
+            pieces = [(s, at + HALF * half) for s in range(16) for half in range(2)]
+            columns.append(jnp.concatenate([in_ref[s, a : a + size, :] for s, a in pieces], axis=0))
+        high, low = split(jnp.concatenate(columns, axis=1))
         two = dot(both, high)
         done = two[:64] + (two[64:] + dot(both[:64], low))
-        for ri in range(2):
-            for q in range(2):
-                j = 2 * ri + q
-                out_ref[pl.ds(ri * 16 + k * 2 + q, 16, stride=32), :] = done[16 * j : 16 * j + 16]
+        for n, k in enumerate(group):
+            for ri in range(2):
+                for q in range(2):
+                    rows = slice(32 * ri + 16 * q, 32 * ri + 16 * q + 16)
+                    out_ref[pl.ds(ri * 16 + k * 2 + q, 16, stride=32), :] = done[
+                        rows, 128 * n : 128 * n + 128
+                    ]
 
 
 def first_kernel(in_ref, tw_ref, table_ref, mix_ref, out_ref):
@@ -262,8 +267,9 @@
         imag = jnp.sum(weight * b2[m : m + 1], axis=1, keepdims=True)
         total = jnp.where(lane == place, real, total)
         total = jnp.where(lane == place + 2, imag, total)
-    for c in range(4):
-        out_ref[pl.ds(c, 16, stride=4), :] = total[16 * c : 16 * c + 16]
+    for c in range(2):
+        two = total[32 * c : 32 * c + 16], total[32 * c + 16 : 32 * c + 32]
+        out_ref[pl.ds(c, 16, stride=2), :] = two[0] + pltpu.roll(two[1], 32, 1)
     b1_ref[...] = b1
     mix = in_ref[4:6]
     for s in range(1, 16):
@@ -282,13 +288,13 @@
 
 
 def first_back_kernel(in_ref, t_ref, mix_ref, out_ref):
-    parts = [in_ref[pl.ds(c, 16, stride=4), :] for c in range(4)]
+    parts = [in_ref[pl.ds(c // 2, 16, stride=2), :] for c in range(4)]
     lane = lanes((16, 128))
     rows = []
     for p in range(2):
         merged = None
         for c in range(4):
-            shift = (16 * (c - p)) % 128
+            shift = (16 * (c - p) - 32 * (c % 2)) % 128
             moved = pltpu.roll(parts[c], shift, 1) if shift else parts[c]
             merged = moved if merged is None else jnp.where((lane // 16) % 4 == c, moved, merged)
         rows.append(merged)
@@ -457,10 +463,10 @@
     spectra = exchange(along_first.reshape(16, 1, 768), "py").reshape(96, 128)
     mode_back, fields, b1, mix = call(
         mode_kernel,
-        (struct(64, 128), struct(64, 128), struct(32, 128), struct(2, 128)),
+        (struct(32, 128), struct(64, 128), struct(32, 128), struct(2, 128)),
         (spectra, spectral_weight.reshape(2048, 128)),
     )
-    mode_back = exchange(mode_back.reshape(16, 4, 128), "py").reshape(64, 128)
+    mode_back = exchange(mode_back.reshape(16, 2, 128), "py").reshape(32, 128)
     spectral_grad = call(
         outer_kernel,
         struct(2048, 128),

time: 121 us -> 121 us (level)
  no operation moved by 1% of the time
where the time goes in v6:
time: 121 us; the launch traced here: 120 us
  blocking collectives  61.6 us (51%)
  waiting for transfers between devices  25.7 us (21%)
  Pallas kernels  19.7 us (16%)
  starting transfers between devices  12.5 us (10%)
    all_to_all x4, blocking collectives, exchange(): return lax.all_to_all(values, axis, split_axis=0, concat_axis=0, tiled=True)  61.6 us
    all_to_all x2, waiting for transfers between devices, exchange(): return lax.all_to_all(values, axis, split_axis=0, concat_axis=0, tiled=True)  25.7 us
    all_to_all x2, starting transfers between devices, exchange(): return lax.all_to_all(values, axis, split_axis=0, concat_axis=0, tiled=True)  12.5 us
    pallas_call x1, Pallas kernels, per_device(): pl.pallas_call(side_kernel, grid=(4,), out_shape=(struct(1024, 512), stru...  7.09 us
    pallas_call x1, Pallas kernels, per_device(): pl.pallas_call(start_kernel, out_shape=struct(N, ROWS, 128), in_specs=[an...  5.36 us
    pallas_call x6, Pallas kernels, call(): pl.pallas_call(body, out_shape=outs, in_specs=whole(len(args)), out_specs...  5.14 us
  transfers between devices with their start and end apart: 2, of which 2 were waited for; matrix products, arithmetic and copies ran while one was open for 0% of the time, Pallas kernels for 7%

profile of v6, /device:TPU:1, one launch (start us, length us, event | category | flops | bytes accessed | tf_op | source)
XLA Modules:
  0.0 120.3 jit_solution(888697851525553564)
XLA Ops:
  0.6 5.4 %shard_map.148 = f32[16,240,128]{2,1,0:T(8,128)} custom-call(f32[4,16,16,512]{3,2,1,0:T(8,128)} %bitcast.27, f32[4,16,16,512]{3,2,1,0:T(8,128)} %bitcast.29, f32[4,16,16,512]{3,2,1,0:T(8,128)} %bitcast.31, bf16[240,256]{1,0:T(8,128)(2,1)} %constant.16.clone.table_ref), custom_call_target="tpu_custom_call" | custom-call | tf_op jit(solution)/shard_map/pallas_call | solution.py:427
  6.0 8.5 %all-to-all-start = ((f32[16,240,128]{2,1,0:T(8,128)}), f32[16,240,128]{2,1,0:T(8,128)S(1)}, u32[]{:S(2)}, u32[]{:S(2)}) async-start(f32[16,240,128]{2,1,0:T(8,128)} %shard_map.148), calls=%async_computation | async-start | bytes 3932160 | tf_op jit(solution)/shard_map/all_to_all | solution.py:415
  14.5 0.0 copy-start.6
  14.5 7.1 %shard_map.149 = (f32[1024,512]{1,0:T(8,128)}, f32[64,128]{1,0:T(8,128)}) custom-call(f32[1024,512]{1,0:T(8,128)} %bitcast.28, f32[1024,512]{1,0:T(8,128)} %bitcast.30, f32[1024,512]{1,0:T(8,128)} %bitcast.32, f32[64,64]{1,0:T(8,128)} %weight_ref.1), custom_call_target="tpu_custom_call" | custom-call | flops 1073741824 | bytes 6291456 | tf_op jit(solution)/shard_map/pallas_call | solution.py:444
  21.6 0.0 copy-start.9
  21.6 0.0 copy-start.1
  21.6 19.9 %all-to-all-done.in_ref = f32[16,240,128]{2,1,0:T(8,128)S(1)} async-done(((f32[16,240,128]{2,1,0:T(8,128)}), f32[16,240,128]{2,1,0:T(8,128)S(1)}, u32[]{:S(2)}, u32[]{:S(2)}) %all-to-all-start) | async-done | bytes 1966112 | tf_op jit(solution)/shard_map/all_to_all | solution.py:415
  41.5 0.0 copy-done.4
  41.5 0.0 copy-done.6
  41.5 0.5 shard_map.150
  42.1 0.0 copy-start.2
  42.1 16.3 %all_to_all.30 = f32[16,32,128]{2,1,0:T(8,128)S(1)} all-to-all(f32[16,32,128]{2,1,0:T(8,128)S(1)} %bitcast.19), channel_id=1, replica_groups=mesh['px'=16,'py'=16] {'px'}, dimensions={0} | all-to-all | bytes 524288 | tf_op jit(solution)/shard_map/all_to_all | solution.py:415
  58.4 0.0 copy-done.7
  58.4 0.0 copy-done.8
  58.4 0.0 copy-done.9
  58.4 0.5 shard_map.151
  58.9 13.7 %all_to_all.31 = f32[16,1,768]{2,1,0:T(1,128)S(1)} all-to-all(f32[16,1,768]{2,1,0:T(1,128)S(1)} %bitcast.24), channel_id=1, replica_groups=mesh['px'=16,'py'=16] {'py'}, dimensions={0} | all-to-all | bytes 98304 | tf_op jit(solution)/shard_map/all_to_all | solution.py:415
  72.6 0.0 copy-done.1
  72.6 0.8 shard_map.152
  73.4 10.1 %all_to_all.32 = f32[16,2,128]{2,1,0:T(2,128)S(1)} all-to-all(f32[16,2,128]{2,1,0:T(2,128)S(1)} %bitcast.26), channel_id=1, replica_groups=mesh['px'=16,'py'=16] {'py'}, dimensions={0} | all-to-all | bytes 32768 | tf_op jit(solution)/shard_map/all_to_all | solution.py:415
  83.5 0.0 copy-done.5
  83.6 1.2 %shard_map.153 = f32[288,128]{1,0:T(8,128)} custom-call(f32[32,128]{1,0:T(8,128)S(1)} %bitcast.25, bf16[192,256]{1,0:T(8,128)(2,1)S(1)} %copy-done.5, f32[2,128]{1,0:T(2,128)S(1)} %get-tuple-element.21.mix_ref), custom_call_target="tpu_custom_call" | custom-call | tf_op jit(solution)/shard_map/pallas_call | solution.py:404
  84.8 4.0 %all-to-all-start.4 = ((f32[16,1,2304]{2,1,0:T(1,128)}), f32[16,1,2304]{2,1,0:T(1,128)S(1)}, u32[]{:S(2)}, u32[]{:S(2)}) async-start(f32[16,1,2304]{2,1,0:T(1,128)} %bitcast.13), calls=%async_computation.4 | async-start | bytes 294912 | tf_op jit(solution)/shard_map/all_to_all | solution.py:415
  88.8 0.0 copy-start
  88.8 0.0 copy-start.3
  88.9 1.7 %shard_map.154 = f32[2048,128]{1,0:T(8,128)} custom-call(f32[64,128]{1,0:T(8,128)S(1)} %get-tuple-element.22.fields_ref, f32[32,128]{1,0:T(8,128)S(1)} %get-tuple-element.23.b1_ref), custom_call_target="tpu_custom_call" | custom-call | flops 1048576 | bytes 1048576 | tf_op jit(solution)/shard_map/pallas_call | solution.py:404
  90.5 5.7 %all-to-all-done.4 = f32[16,1,2304]{2,1,0:T(1,128)S(1)} async-done(((f32[16,1,2304]{2,1,0:T(1,128)}), f32[16,1,2304]{2,1,0:T(1,128)S(1)}, u32[]{:S(2)}, u32[]{:S(2)}) %all-to-all-start.4) | async-done | bytes 147488 | tf_op jit(solution)/shard_map/all_to_all | solution.py:415
  96.3 0.0 copy-done.2
  96.3 0.4 shard_map.155
  96.7 21.4 %all_to_all.33.in_ref = f32[16,128,128]{2,1,0:T(8,128)S(1)} all-to-all(f32[16,128,128]{2,1,0:T(8,128)S(1)} %shard_map.155), channel_id=1, replica_groups=mesh['px'=16,'py'=16] {'py'}, dimensions={0} | all-to-all | bytes 2097152 | tf_op jit(solution)/shard_map/all_to_all | solution.py:415
  118.2 0.0 copy-done
  118.2 2.1 %shard_map.156 = (f32[4,16,16,512]{3,2,1,0:T(8,128)}, f32[64,64]{1,0:T(8,128)}) custom-call(f32[16,128,128]{2,1,0:T(8,128)S(1)} %all_to_all.33.in_ref, f32[4,16,16,512]{3,2,1,0:T(8,128)S(1)} %bitcast.18, bf16[256,256]{1,0:T(8,128)(2,1)S(1)} %copy-done.3), custom_call_target="tpu_custom_call" | custom-call | tf_op jit(solution)/shard_map/pallas_call | solution.py:490
  (5 shorter events, 0.0 us)
Async XLA Ops:
  6.0 35.5 %all-to-all-start = ((f32[16,240,128]{2,1,0:T(8,128)}), f32[16,240,128]{2,1,0:T(8,128)S(1)}, u32[]{:S(2)}, u32[]{:S(2)}) async-start(f32[16,240,128]{2,1,0:T(8,128)} %shard_map.148), calls=%async_computation | async-start | bytes 3932160 | tf_op jit(solution)/shard_map/all_to_all | solution.py:415
  14.5 27.1 %copy-start.4 = (bf16[128,512]{1,0:T(8,128)(2,1)S(1)}, bf16[128,512]{1,0:T(8,128)(2,1)}, u32[]{:S(2)}) copy-start(bf16[128,512]{1,0:T(8,128)(2,1)} %constant.17.clone.table_ref) | copy-start | bytes 393220
  14.5 27.1 %copy-start.6 = (bf16[128,256]{1,0:T(8,128)(2,1)S(1)}, bf16[128,256]{1,0:T(8,128)(2,1)}, u32[]{:S(2)}) copy-start(bf16[128,256]{1,0:T(8,128)(2,1)} %constant.18.clone.real_ref) | copy-start | bytes 196612
  21.6 36.8 %copy-start.7 = (bf16[64,256]{1,0:T(8,128)(2,1)S(1)}, bf16[64,256]{1,0:T(8,128)(2,1)}, u32[]{:S(2)}) copy-start(bf16[64,256]{1,0:T(8,128)(2,1)} %constant.20.clone.table_ref) | copy-start | bytes 98308
  21.6 36.8 %copy-start.8 = (f32[64,128]{1,0:T(8,128)S(1)}, f32[64,128]{1,0:T(8,128)}, u32[]{:S(2)}) copy-start(f32[64,128]{1,0:T(8,128)} %get-tuple-element.19.mix_ref) | copy-start | bytes 98308
  21.6 36.8 %copy-start.9 = (f32[32,128]{1,0:T(8,128)S(1)}, f32[32,128]{1,0:T(8,128)}, u32[]{:S(2)}) copy-start(f32[32,128]{1,0:T(8,128)} %constant.19.clone.tw_ref) | copy-start | bytes 49156
  21.6 51.0 %copy-start.1 = (f32[2,2,8,64,128]{4,3,2,1,0:T(8,128)S(1)}, f32[2,2,8,64,128]{4,3,2,1,0:T(8,128)}, u32[]{:S(2)}) copy-start(f32[2,2,8,64,128]{4,3,2,1,0:T(8,128)} %param.17) | copy-start | bytes 3145732
  41.5 42.0 %copy-start.5 = (bf16[192,256]{1,0:T(8,128)(2,1)S(1)}, bf16[192,256]{1,0:T(8,128)(2,1)}, u32[]{:S(2)}) copy-start(bf16[192,256]{1,0:T(8,128)(2,1)} %constant.21.clone.t_ref) | copy-start | bytes 294916
  42.1 54.2 %copy-start.2 = (bf16[512,192]{1,0:T(8,128)(2,1)S(1)}, bf16[512,192]{1,0:T(8,128)(2,1)}, u32[]{:S(2)}) copy-start(bf16[512,192]{1,0:T(8,128)(2,1)} %constant.22.clone.t_ref) | copy-start | bytes 589828
  84.8 11.5 %all-to-all-start.4 = ((f32[16,1,2304]{2,1,0:T(1,128)}), f32[16,1,2304]{2,1,0:T(1,128)S(1)}, u32[]{:S(2)}, u32[]{:S(2)}) async-start(f32[16,1,2304]{2,1,0:T(1,128)} %bitcast.13), calls=%async_computation.4 | async-start | bytes 294912 | tf_op jit(solution)/shard_map/all_to_all | solution.py:415
  88.8 29.3 %copy-start = (f32[1024,512]{1,0:T(8,128)S(1)}, f32[1024,512]{1,0:T(8,128)}, u32[]{:S(2)}) copy-start(f32[1024,512]{1,0:T(8,128)} %get-tuple-element.25) | copy-start | bytes 6291460
  88.8 29.3 %copy-start.3 = (bf16[256,256]{1,0:T(8,128)(2,1)S(1)}, bf16[256,256]{1,0:T(8,128)(2,1)}, u32[]{:S(2)}) copy-start(bf16[256,256]{1,0:T(8,128)(2,1)} %constant.23.clone.table_ref) | copy-start | bytes 393220

commit v7 on v6

--- a/solution.py
+++ b/solution.py
@@ -190,10 +190,10 @@
             for half in range(2):
                 high, low = split(rows[:, 256 * half : 256 * half + 256])
                 two = dot(both, high, ((1,), (1,)))
-                done = two[:HALF] + (two[HALF:] + dot(both[:HALF], low, ((1,), (1,))))
+                done = two[:128] + (two[128:] + dot(both[:128], low, ((1,), (1,))))
                 for n in range(2):
                     at = slice(HALF * half, HALF * half + HALF)
-                    out[first + j + n, at] = done[:, 128 * n : 128 * n + 128]
+                    out[first + j + n, at] = done[:HALF, 128 * n : 128 * n + 128]
         at = pl.ds(first, size)
         send = pltpu.make_async_copy(out.at[at], out_hbm.at[at], out_sems.at[i])
         send.start()
@@ -438,7 +438,7 @@
             pltpu.SemaphoreType.DMA((len(START_PARTS),)),
         ],
         compiler_params=params(60),
-    )(*shaped, column(depth_sent()))
+    )(*shaped, column(np.pad(depth_sent(), ((0, 128 - HALF), (0, 0)))))
 
     tile_spec = pl.BlockSpec((1024, 128), lambda i: (0, i))
     direct, mix = pl.pallas_call(

time: 121 us -> 121 us (level)
  no operation moved by 1% of the time
where the time goes in v7:
time: 121 us; the launch traced here: 120 us
  blocking collectives  61.6 us (51%)
  waiting for transfers between devices  25.7 us (21%)
  Pallas kernels  19.7 us (16%)
  starting transfers between devices  12.5 us (10%)
    all_to_all x4, blocking collectives, exchange(): return lax.all_to_all(values, axis, split_axis=0, concat_axis=0, tiled=True)  61.6 us
    all_to_all x2, waiting for transfers between devices, exchange(): return lax.all_to_all(values, axis, split_axis=0, concat_axis=0, tiled=True)  25.7 us
    all_to_all x2, starting transfers between devices, exchange(): return lax.all_to_all(values, axis, split_axis=0, concat_axis=0, tiled=True)  12.5 us
    pallas_call x1, Pallas kernels, per_device(): pl.pallas_call(side_kernel, grid=(4,), out_shape=(struct(1024, 512), stru...  7.09 us
    pallas_call x1, Pallas kernels, per_device(): pl.pallas_call(start_kernel, out_shape=struct(N, ROWS, 128), in_specs=[an...  5.39 us
    pallas_call x6, Pallas kernels, call(): pl.pallas_call(body, out_shape=outs, in_specs=whole(len(args)), out_specs...  5.14 us
  transfers between devices with their start and end apart: 2, of which 2 were waited for; matrix products, arithmetic and copies ran while one was open for 0% of the time, Pallas kernels for 7%

profile of v7, /device:TPU:1, one launch (start us, length us, event | category | flops | bytes accessed | tf_op | source)
XLA Modules:
  0.0 120.3 jit_solution(6281404569208217075)
XLA Ops:
  0.6 5.4 %shard_map.148 = f32[16,240,128]{2,1,0:T(8,128)} custom-call(f32[4,16,16,512]{3,2,1,0:T(8,128)} %bitcast.27, f32[4,16,16,512]{3,2,1,0:T(8,128)} %bitcast.29, f32[4,16,16,512]{3,2,1,0:T(8,128)} %bitcast.31, bf16[256,256]{1,0:T(8,128)(2,1)} %constant.16.clone.table_ref), custom_call_target="tpu_custom_call" | custom-call | tf_op jit(solution)/shard_map/pallas_call | solution.py:427
  6.0 8.5 %all-to-all-start = ((f32[16,240,128]{2,1,0:T(8,128)}), f32[16,240,128]{2,1,0:T(8,128)S(1)}, u32[]{:S(2)}, u32[]{:S(2)}) async-start(f32[16,240,128]{2,1,0:T(8,128)} %shard_map.148), calls=%async_computation | async-start | bytes 3932160 | tf_op jit(solution)/shard_map/all_to_all | solution.py:415
  14.5 0.0 copy-start.6
  14.5 7.1 %shard_map.149 = (f32[1024,512]{1,0:T(8,128)}, f32[64,128]{1,0:T(8,128)}) custom-call(f32[1024,512]{1,0:T(8,128)} %bitcast.28, f32[1024,512]{1,0:T(8,128)} %bitcast.30, f32[1024,512]{1,0:T(8,128)} %bitcast.32, f32[64,64]{1,0:T(8,128)} %weight_ref.1), custom_call_target="tpu_custom_call" | custom-call | flops 1073741824 | bytes 6291456 | tf_op jit(solution)/shard_map/pallas_call | solution.py:444
  21.6 0.0 copy-start.9
  21.6 0.0 copy-start.1
  21.6 19.9 %all-to-all-done.in_ref = f32[16,240,128]{2,1,0:T(8,128)S(1)} async-done(((f32[16,240,128]{2,1,0:T(8,128)}), f32[16,240,128]{2,1,0:T(8,128)S(1)}, u32[]{:S(2)}, u32[]{:S(2)}) %all-to-all-start) | async-done | bytes 1966112 | tf_op jit(solution)/shard_map/all_to_all | solution.py:415
  41.6 0.0 copy-done.4
  41.6 0.0 copy-done.6
  41.6 0.5 shard_map.150
  42.1 0.0 copy-start.2
  42.1 16.3 %all_to_all.30 = f32[16,32,128]{2,1,0:T(8,128)S(1)} all-to-all(f32[16,32,128]{2,1,0:T(8,128)S(1)} %bitcast.19), channel_id=1, replica_groups=mesh['px'=16,'py'=16] {'px'}, dimensions={0} | all-to-all | bytes 524288 | tf_op jit(solution)/shard_map/all_to_all | solution.py:415
  58.4 0.0 copy-done.7
  58.4 0.0 copy-done.8
  58.4 0.0 copy-done.9
  58.4 0.5 shard_map.151
  58.9 13.7 %all_to_all.31 = f32[16,1,768]{2,1,0:T(1,128)S(1)} all-to-all(f32[16,1,768]{2,1,0:T(1,128)S(1)} %bitcast.24), channel_id=1, replica_groups=mesh['px'=16,'py'=16] {'py'}, dimensions={0} | all-to-all | bytes 98304 | tf_op jit(solution)/shard_map/all_to_all | solution.py:415
  72.6 0.0 copy-done.1
  72.7 0.8 shard_map.152
  73.5 10.1 %all_to_all.32 = f32[16,2,128]{2,1,0:T(2,128)S(1)} all-to-all(f32[16,2,128]{2,1,0:T(2,128)S(1)} %bitcast.26), channel_id=1, replica_groups=mesh['px'=16,'py'=16] {'py'}, dimensions={0} | all-to-all | bytes 32768 | tf_op jit(solution)/shard_map/all_to_all | solution.py:415
  83.6 0.0 copy-done.5
  83.6 1.2 %shard_map.153 = f32[288,128]{1,0:T(8,128)} custom-call(f32[32,128]{1,0:T(8,128)S(1)} %bitcast.25, bf16[192,256]{1,0:T(8,128)(2,1)S(1)} %copy-done.5, f32[2,128]{1,0:T(2,128)S(1)} %get-tuple-element.21.mix_ref), custom_call_target="tpu_custom_call" | custom-call | tf_op jit(solution)/shard_map/pallas_call | solution.py:404
  84.8 4.0 %all-to-all-start.4 = ((f32[16,1,2304]{2,1,0:T(1,128)}), f32[16,1,2304]{2,1,0:T(1,128)S(1)}, u32[]{:S(2)}, u32[]{:S(2)}) async-start(f32[16,1,2304]{2,1,0:T(1,128)} %bitcast.13), calls=%async_computation.4 | async-start | bytes 294912 | tf_op jit(solution)/shard_map/all_to_all | solution.py:415
  88.9 0.0 copy-start
  88.9 0.0 copy-start.3
  88.9 1.7 %shard_map.154 = f32[2048,128]{1,0:T(8,128)} custom-call(f32[64,128]{1,0:T(8,128)S(1)} %get-tuple-element.22.fields_ref, f32[32,128]{1,0:T(8,128)S(1)} %get-tuple-element.23.b1_ref), custom_call_target="tpu_custom_call" | custom-call | flops 1048576 | bytes 1048576 | tf_op jit(solution)/shard_map/pallas_call | solution.py:404
  90.6 5.7 %all-to-all-done.4 = f32[16,1,2304]{2,1,0:T(1,128)S(1)} async-done(((f32[16,1,2304]{2,1,0:T(1,128)}), f32[16,1,2304]{2,1,0:T(1,128)S(1)}, u32[]{:S(2)}, u32[]{:S(2)}) %all-to-all-start.4) | async-done | bytes 147488 | tf_op jit(solution)/shard_map/all_to_all | solution.py:415
  96.3 0.0 copy-done.2
  96.3 0.4 shard_map.155
  96.7 21.4 %all_to_all.33.in_ref = f32[16,128,128]{2,1,0:T(8,128)S(1)} all-to-all(f32[16,128,128]{2,1,0:T(8,128)S(1)} %shard_map.155), channel_id=1, replica_groups=mesh['px'=16,'py'=16] {'py'}, dimensions={0} | all-to-all | bytes 2097152 | tf_op jit(solution)/shard_map/all_to_all | solution.py:415
  118.2 0.0 copy-done.3
  118.2 2.1 %shard_map.156 = (f32[4,16,16,512]{3,2,1,0:T(8,128)}, f32[64,64]{1,0:T(8,128)}) custom-call(f32[16,128,128]{2,1,0:T(8,128)S(1)} %all_to_all.33.in_ref, f32[4,16,16,512]{3,2,1,0:T(8,128)S(1)} %bitcast.18, bf16[256,256]{1,0:T(8,128)(2,1)S(1)} %copy-done.3), custom_call_target="tpu_custom_call" | custom-call | tf_op jit(solution)/shard_map/pallas_call | solution.py:490
  (5 shorter events, 0.0 us)
Async XLA Ops:
  6.0 35.5 %all-to-all-start = ((f32[16,240,128]{2,1,0:T(8,128)}), f32[16,240,128]{2,1,0:T(8,128)S(1)}, u32[]{:S(2)}, u32[]{:S(2)}) async-start(f32[16,240,128]{2,1,0:T(8,128)} %shard_map.148), calls=%async_computation | async-start | bytes 3932160 | tf_op jit(solution)/shard_map/all_to_all | solution.py:415
  14.5 27.1 %copy-start.4 = (bf16[128,512]{1,0:T(8,128)(2,1)S(1)}, bf16[128,512]{1,0:T(8,128)(2,1)}, u32[]{:S(2)}) copy-start(bf16[128,512]{1,0:T(8,128)(2,1)} %constant.17.clone.table_ref) | copy-start | bytes 393220
  14.5 27.1 %copy-start.6 = (bf16[128,256]{1,0:T(8,128)(2,1)S(1)}, bf16[128,256]{1,0:T(8,128)(2,1)}, u32[]{:S(2)}) copy-start(bf16[128,256]{1,0:T(8,128)(2,1)} %constant.18.clone.real_ref) | copy-start | bytes 196612
  21.6 36.8 %copy-start.7 = (bf16[64,256]{1,0:T(8,128)(2,1)S(1)}, bf16[64,256]{1,0:T(8,128)(2,1)}, u32[]{:S(2)}) copy-start(bf16[64,256]{1,0:T(8,128)(2,1)} %constant.20.clone.table_ref) | copy-start | bytes 98308
  21.6 36.8 %copy-start.8 = (f32[64,128]{1,0:T(8,128)S(1)}, f32[64,128]{1,0:T(8,128)}, u32[]{:S(2)}) copy-start(f32[64,128]{1,0:T(8,128)} %get-tuple-element.19.mix_ref) | copy-start | bytes 98308
  21.6 36.8 %copy-start.9 = (f32[32,128]{1,0:T(8,128)S(1)}, f32[32,128]{1,0:T(8,128)}, u32[]{:S(2)}) copy-start(f32[32,128]{1,0:T(8,128)} %constant.19.clone.tw_ref) | copy-start | bytes 49156
  21.6 51.0 %copy-start.1 = (f32[2,2,8,64,128]{4,3,2,1,0:T(8,128)S(1)}, f32[2,2,8,64,128]{4,3,2,1,0:T(8,128)}, u32[]{:S(2)}) copy-start(f32[2,2,8,64,128]{4,3,2,1,0:T(8,128)} %param.17) | copy-start | bytes 3145732
  41.6 42.0 %copy-start.5 = (bf16[192,256]{1,0:T(8,128)(2,1)S(1)}, bf16[192,256]{1,0:T(8,128)(2,1)}, u32[]{:S(2)}) copy-start(bf16[192,256]{1,0:T(8,128)(2,1)} %constant.21.clone.t_ref) | copy-start | bytes 294916
  42.1 54.2 %copy-start.2 = (bf16[512,192]{1,0:T(8,128)(2,1)S(1)}, bf16[512,192]{1,0:T(8,128)(2,1)}, u32[]{:S(2)}) copy-start(bf16[512,192]{1,0:T(8,128)(2,1)} %constant.22.clone.t_ref) | copy-start | bytes 589828
  84.8 11.5 %all-to-all-start.4 = ((f32[16,1,2304]{2,1,0:T(1,128)}), f32[16,1,2304]{2,1,0:T(1,128)S(1)}, u32[]{:S(2)}, u32[]{:S(2)}) async-start(f32[16,1,2304]{2,1,0:T(1,128)} %bitcast.13), calls=%async_computation.4 | async-start | bytes 294912 | tf_op jit(solution)/shard_map/all_to_all | solution.py:415
  88.9 29.3 %copy-start = (f32[1024,512]{1,0:T(8,128)S(1)}, f32[1024,512]{1,0:T(8,128)}, u32[]{:S(2)}) copy-start(f32[1024,512]{1,0:T(8,128)} %get-tuple-element.25) | copy-start | bytes 6291460
  88.9 29.3 %copy-start.3 = (bf16[256,256]{1,0:T(8,128)(2,1)S(1)}, bf16[256,256]{1,0:T(8,128)(2,1)}, u32[]{:S(2)}) copy-start(bf16[256,256]{1,0:T(8,128)(2,1)} %constant.23.clone.table_ref) | copy-start | bytes 393220
